TPU v7x, 256 devices: a whole 4x4x8 slice. The times are simulated.
256 devices in a mesh: dp: 16 (over x_hi, z), tensor: 16 (over y, x_lo, core).
Axes of the slice: x: 4 (x_hi: 2, x_lo: 2; x = x_hi * 2 + x_lo), y: 4, z: 8, core: 2. Of those that a mesh axis runs over, the one named last changes fastest.
Arguments:
- hidden_in: bfloat16 [4096, 12288], P('dp', 'tensor'), as said below
- residual_grad: bfloat16 [4096, 12288], P('dp', 'tensor'), may hold values from -6 to 6
- key_value_gradient: bfloat16 [4096, 2048], P('dp', 'tensor'), as said below
- shortcut: bfloat16 [12288, 12288], P('dp', 'tensor'), may hold values from -0.02734375 to 0.02734375
- key_value_weight: bfloat16 [12288, 2048], P('dp', 'tensor'), as said below
- adapter_down_matrix: float32 [12288, 64], replicated, may hold values from -0.0546875 to 0.0546875
- adapter_up: float32 [64, 2048], replicated, may hold values from -0.75 to 0.75
Outputs:
- input_grad: bfloat16 [4096, 12288], P(('dp', 'tensor'))
- adapter_down_grad: float32 [12288, 64], replicated
- adapter_up_grad: float32 [64, 2048], replicated
Inputs may be any that keep to these rules, and one draw needn't show every extreme that they name: `hidden_in`: entries are finite; token rows and feature columns have unlike scales. `key_value_gradient`: entries are finite. `key_value_weight`: entries are finite.
All inputs are finite; a program needn't handle non-finite values.
Results may differ from a plain program's by a relative error of at most 0.0095.
Values may be sent and summed in bfloat16 or wider, within the bound.
A program may use at most 128 MiB of HBM per device.

v0:
```python
import jax
import jax.numpy as jnp
from jax import lax
from jax.sharding import PartitionSpec as P

epsilon = 1e-05
adapter_scale = 0.25


def contract_final_axis(left, right):
    return lax.dot_general(
        left, right, (((1,), (1,)), ((), ())), preferred_element_type=jnp.float32
    )


def shards(
    hidden_in,
    residual_grad,
    key_value_gradient,
    shortcut,
    key_value_weight,
    adapter_down_matrix,
    adapter_up,
):
    highest_precision = lax.Precision.HIGHEST
    tensor_count = lax.axis_size("tensor")
    lane_index = lax.axis_index("tensor")
    group_rows = hidden_in.shape[0]
    feat_lane = hidden_in.shape[1]
    kv_lane = key_value_gradient.shape[1]
    features = adapter_down_matrix.shape[0]
    rank_width = adapter_down_matrix.shape[1]
    row_block = group_rows // tensor_count
    inputs32 = hidden_in.astype(jnp.float32)
    key_value_float32 = key_value_gradient.astype(jnp.float32)
    down_rows = lax.dynamic_slice_in_dim(adapter_down_matrix, lane_index * feat_lane, feat_lane, 0)
    up_columns = lax.dynamic_slice_in_dim(adapter_up, lane_index * kv_lane, kv_lane, 1)
    partial_down = jnp.dot(inputs32, down_rows, precision=highest_precision)
    partial_back = jnp.dot(key_value_float32, up_columns.T, precision=highest_precision)
    partial_squares = jnp.sum(inputs32 * inputs32, axis=1)
    short_cols, kv_cols = (
        lax.all_gather(shortcut, "dp", axis=0, tiled=True),
        lax.all_gather(key_value_weight, "dp", axis=0, tiled=True),
    )
    summed_down, backward_value, squares = lax.psum(
        (partial_down, partial_back, partial_squares), "tensor"
    )
    token_rows = lax.all_to_all(hidden_in, "tensor", split_axis=0, concat_axis=1, tiled=True)
    scale_row = lax.rsqrt(squares / features + epsilon)
    low_rank_product = scale_row[:, None] * summed_down
    up_shard_local = adapter_scale * jnp.dot(
        low_rank_product.T, key_value_float32, precision=highest_precision
    )
    normalized_local = inputs32 * scale_row[:, None]
    down_shard_local = adapter_scale * jnp.dot(
        normalized_local.T, backward_value, precision=highest_precision
    )
    shortcut_term = contract_final_axis(residual_grad, short_cols)
    norm_term = contract_final_axis(key_value_gradient, kv_cols)
    combined = lax.psum_scatter(
        jnp.concatenate([shortcut_term, norm_term], axis=1),
        "tensor",
        scatter_dimension=0,
        tiled=True,
    )
    short_part = combined[:, :features]
    norm_portion = combined[:, features:]
    my_scale = lax.dynamic_slice_in_dim(scale_row, lane_index * row_block, row_block, 0)
    local_backward = lax.dynamic_slice_in_dim(backward_value, lane_index * row_block, row_block, 0)
    normalized_input = token_rows.astype(jnp.float32) * my_scale[:, None]
    adapter_term = adapter_scale * jnp.dot(
        local_backward, adapter_down_matrix.T, precision=highest_precision
    )
    gradient_norm = norm_portion + adapter_term
    inner = jnp.mean(gradient_norm * normalized_input, axis=1, keepdims=True)
    result = short_part + my_scale[:, None] * (gradient_norm - normalized_input * inner)
    down_full = lax.dynamic_update_slice(
        jnp.zeros((features, rank_width), jnp.float32),
        down_shard_local,
        (lane_index * feat_lane, 0),
    )
    up_full = lax.dynamic_update_slice(
        jnp.zeros((rank_width, kv_lane * tensor_count), jnp.float32),
        up_shard_local,
        (0, lane_index * kv_lane),
    )
    down_gradient, up_gradient = lax.psum((down_full, up_full), ("dp", "tensor"))
    return (result.astype(jnp.bfloat16), down_gradient, up_gradient)


def solution(mesh):
    in_specs = (
        P("dp", "tensor"),
        P("dp", "tensor"),
        P("dp", "tensor"),
        P("dp", "tensor"),
        P("dp", "tensor"),
        P(),
        P(),
    )
    out_specs = (P(("dp", "tensor"), None), P(), P())
    return jax.shard_map(shards, mesh=mesh, in_specs=in_specs, out_specs=out_specs, check_vma=False)
```

profile of v0, /device:TPU:1, one launch (start us, length us, event | category | flops | bytes accessed | tf_op | source)
XLA Modules:
  0.0 936.7 jit_solution(15242859219998327507)
XLA Ops:
  8.0 0.0 copy-start
  8.0 0.0 all-gather.5.cloned.1.call-start
  8.1 0.7 all-gather.5.cloned.1.call-update
  8.7 0.0 all-gather.3.cloned.1.call-start
  8.8 0.7 all-gather.3.cloned.1.call-update
  9.5 0.0 all-reduce.7.cloned.1.call-start
  9.6 1.7 convolution_bitcast_fusion.1
  11.3 0.0 copy-done
  11.3 2.1 convolution_bitcast_fusion
  13.4 0.0 all-reduce.7.cloned.1.call-update
  13.4 0.0 copy-start.4
  13.4 0.0 reduce-scatter.2.cloned.1.call-start
  13.5 92.0 %all-gather.5.cloned.1.call-done = bf16[12288,128]{1,0:T(8,128)(2,1)} async-done(((bf16[768,128]{1,0:T(8,128)(2,1)}), bf16[12288,128]{1,0:T(8,128)(2,1)}) %all-gather.5.cloned.1.call-update) | async-done | bytes 3145744 | tf_op jit(solution)/shard_map/all_gather | solution.py:43
  105.5 8.3 fusion.15
  113.9 243.0 %all-gather.3.cloned.1.call-done = bf16[12288,768]{1,0:T(8,128)(2,1)} async-done(((bf16[768,768]{1,0:T(8,128)(2,1)}), bf16[12288,768]{1,0:T(8,128)(2,1)}) %all-gather.3.cloned.1.call-update) | async-done | bytes 18874384 | tf_op jit(solution)/shard_map/all_gather | solution.py:42
  356.9 0.0 copy-done.4
  356.9 11.6 %fusion.14 = f32[256,12288]{1,0:T(8,128)} fusion(bf16[256,768]{1,0:T(8,128)(2,1)S(1)} %copy-done.4, bf16[12288,768]{1,0:T(8,128)(2,1)} %all-gather.3.cloned.1.call-done), kind=kOutput, calls=%fused_computation.27 | convolution fusion | flops 4831838208 | bytes 31850496 | tf_op jit(solution)/shard_map/dot_general | solution.py:11
  368.5 18.3 %pad_maximum_fusion = f32[256,24576]{1,0:T(8,128)} fusion(f32[256,12288]{1,0:T(8,128)} %fusion.15, f32[256,12288]{1,0:T(8,128)} %fusion.14), kind=kLoop, calls=%fused_computation | loop fusion | flops 6291456 | bytes 50331648 | tf_op jit(solution)/shard_map/concatenate | solution.py:61
  386.8 0.0 reduce-scatter.2.cloned.1.call-update
  386.8 5.4 all-to-all-start
  392.2 0.0 all-reduce.5.cloned.1.call-start
  392.3 1.2 fusion.3
  393.5 30.0 %psum.35 = f32[256]{0:T(256)S(1)} all-reduce(f32[256]{0:T(256)S(1)} %fusion.3), channel_id=1, replica_groups=mesh['dp'=16,'tensor'=16] {'tensor'}, use_global_device_ids=true, to_apply=%region_2.0 | all-reduce | flops 256 | bytes 2048 | tf_op jit(solution)/shard_map/psum | solution.py:45
  423.4 0.1 dynamic_slice.12
  423.5 0.0 all-reduce.7.cloned.1.call-done
  423.5 0.0 copy-start.5
  423.5 0.8 broadcast_in_dim.5
  424.3 1.9 fusion.2
  426.2 1.9 broadcast_in_dim.4
  428.1 0.0 copy-done.5
  428.1 2.4 fusion.1
  430.5 0.0 all-reduce.5.cloned.1.call-update
  430.6 0.0 all-to-all-done
  430.6 0.1 convert_bitcast_fusion
  430.7 1.0 copy.12
  431.6 222.7 %reduce-scatter.2.cloned.1.call-done = f32[16,24576]{1,0:T(8,128)} async-done(((f32[256,24576]{1,0:T(8,128)}), f32[16,24576]{1,0:T(8,128)}) %reduce-scatter.2.cloned.1.call-update) | async-done | bytes 1572880 | tf_op jit(solution)/shard_map/reduce_scatter | solution.py:60
  654.3 0.0 copy-start.1
  654.3 0.0 copy-start.2
  654.3 3.3 multiply_reduce_fusion
  657.6 0.0 copy-done.1
  657.7 0.0 copy-done.2
  657.7 1.0 fusion.4
  658.6 265.9 %all-reduce.5.cloned.1.call-done = (f32[12288,64]{0,1:T(8,128)}, f32[64,2048]{1,0:T(8,128)}) async-done(((f32[12288,64]{0,1:T(8,128)}, f32[64,2048]{1,0:T(8,128)}), (f32[12288,64]{0,1:T(8,128)}, f32[64,2048]{1,0:T(8,128)})) %all-reduce.5.cloned.1.call-update) | async-done | bytes 3670032 | tf_op jit(solution)/shard_map/psum | solution.py:87
  924.5 0.0 copy-start.3
  924.5 3.8 copy.19
  928.4 0.0 copy-done.3
  928.4 0.8 copy.20
  (2 shorter events, 0.0 us)
Async XLA Ops:
  8.0 3.3 copy-start
  8.0 97.5 %all-gather.5.cloned.1.call-start = ((), (), s32[]{:S(2)}) async-start(), calls=%async_computation.3 | async-start | bytes 3342336 | tf_op jit(solution)/shard_map/all_gather | solution.py:43
  8.7 348.1 %all-gather.3.cloned.1.call-start = ((), (), s32[]{:S(2)}) async-start(), calls=%async_computation.2 | async-start | bytes 20054016 | tf_op jit(solution)/shard_map/all_gather | solution.py:42
  9.5 414.0 %all-reduce.7.cloned.1.call-start = ((), (), s32[]{:S(2)}) async-start(), calls=%async_computation.6 | async-start | bytes 393216 | tf_op jit(solution)/shard_map/psum | solution.py:45
  13.4 343.5 %copy-start.4 = (bf16[256,768]{1,0:T(8,128)(2,1)S(1)}, bf16[256,768]{1,0:T(8,128)(2,1)}, u32[]{:S(2)}) copy-start(bf16[256,768]{1,0:T(8,128)(2,1)} %param.8) | copy-start | bytes 1179652
  13.4 640.9 %reduce-scatter.2.cloned.1.call-start = ((), (), s32[]{:S(2)}) async-start(), calls=%async_computation.4 | async-start | bytes 26738688 | tf_op jit(solution)/shard_map/reduce_scatter | solution.py:60
  386.8 43.8 %all-to-all-start = ((bf16[16,16,768]{2,1,0:T(8,128)(2,1)}), bf16[16,16,768]{2,1,0:T(8,128)(2,1)S(1)}, u32[]{:S(2)}, u32[]{:S(2)}) async-start(bf16[16,16,768]{2,1,0:T(8,128)(2,1)} %bitcast.1), calls=%async_computation.1 | async-start | bytes 786432 | tf_op jit(solution)/shard_map/all_to_all | solution.py:48
  392.2 532.3 %all-reduce.5.cloned.1.call-start = ((), (), s32[]{:S(2)}) async-start(), calls=%async_computation.5 | async-start | bytes 7340032 | tf_op jit(solution)/shard_map/psum | solution.py:87
  423.5 4.6 copy-start.5
  654.3 3.3 copy-start.1
  654.3 3.3 copy-start.2
  924.5 3.8 copy-start.3
Sparse Core Ops, SparseCore 0:
  11.8 93.6 all-gather.4
  108.4 248.3 all-gather.2
Sparse Core Ops, SparseCore 1:
  13.5 143.8 all-reduce.6
  386.9 267.4 reduce-scatter.1
  661.3 263.2 all-reduce.4
where the time goes:
time: 938 us; the launch traced here: 937 us
  waiting for transfers between devices  825 us (88%)
  matrix products  31.4 us (3%)
  blocking collectives  30 us (3%)
  other arithmetic  20.5 us (2%)
  between operations  15.7 us (2%)
    psum x1, waiting for transfers between devices, shards(): lax.psum((down_full, up_full), ('dp', 'tensor'))  266 us
    all_gather x1, waiting for transfers between devices, shards(): lax.all_gather(shortcut, 'dp', axis=0, tiled=True)  243 us
    reduce_scatter x1, waiting for transfers between devices, shards(): lax.psum_scatter(jnp.concatenate([shortcut_term, norm_term], axis=1), 'te...  223 us
    all_gather x1, waiting for transfers between devices, shards(): lax.all_gather(key_value_weight, 'dp', axis=0, tiled=True)  92 us
    psum x1, blocking collectives, shards(): lax.psum((partial_down, partial_back, partial_squares), 'tensor')  30 us
    dot_general x2, matrix products, contract_final_axis(): lax.dot_general(left, right, (((1,), (1,)), ((), ())), preferred_element_...  20 us
  transfers between devices with their start and end apart: 6, of which 4 were waited for; matrix products, arithmetic and copies ran while one was open for 6% of the time, Pallas kernels for 0%

commit v1 on v0

v1 whole, which is shorter than its diff:
```python
import jax
import jax.numpy as jnp
from jax import lax
from jax.experimental import pallas as pl
from jax.experimental.pallas import tpu as pltpu
from jax.sharding import PartitionSpec as P

MESH = pl.DeviceIdType.MESH
UNITS = 16
LAG = 2
PIECES = 4


def place(xh, z, y, xl, c):
    return {"dp": xh * 8 + z, "tensor": (y * 2 + xl) * 2 + c}


def contract(a, b):
    return lax.dot_general(a, b, (((1,), (1,)), ((), ())), preferred_element_type=jnp.float32)


def short_kernel(
    grad_ref, short_ref, out_ref,
    blocks, weights, relay, core_out, core_in, own, y_out, y_in, pair, x_out, x_in, fin_out, fin_in,
    load_sem, a_send, a_recv, s_send, s_recv, r_send, r_recv,
    core_send, core_recv, y_send, y_recv, x_send, x_recv, f_send, f_recv,
):
    p, q = lax.axis_index("dp"), lax.axis_index("tensor")
    xh, z = p // 8, p % 8
    y, xl, c = q // 4, (q // 2) % 2, q % 2
    x = xh * 2 + xl
    xp, xm = (x + 1) % 4, (x + 3) % 4

    def at(xh=xh, z=z, y=y, xl=xl, c=c):
        return place(xh, z, y, xl, c)

    right, left = at(xh=xp // 2, xl=xp % 2), at(xh=xm // 2, xl=xm % 2)
    up, down = at(z=(z + 1) % 8), at(z=(z + 7) % 8)
    core_peer = at(c=1 - c)
    xl_peer = at(xl=1 - xl)

    loads = [pltpu.make_async_copy(grad_ref.at[:, h], blocks.at[0, h], load_sem.at[h]) for h in range(2)]
    loads.append(pltpu.make_async_copy(short_ref, weights.at[0], load_sem.at[2]))
    for l in loads:
        l.start()

    barrier = pltpu.get_barrier_semaphore()
    peers = [core_peer, right, left] + [at(y=(y + d) % 4) for d in (1, 2, 3)] + [at(z=(z + d) % 8) for d in range(1, 8)]
    for peer in peers:
        pl.semaphore_signal(barrier, inc=1, device_id=peer, device_id_type=MESH)
    for l in loads:
        l.wait()
    pl.semaphore_wait(barrier, len(peers))

    def remote(src, dst, send, recv, to):
        return pltpu.make_async_remote_copy(
            src_ref=src, dst_ref=dst, send_sem=send, recv_sem=recv, device_id=to, device_id_type=MESH
        )

    rows = 384 // PIECES

    def swap_copy(way, n):
        lo = way * 384 + n * rows
        i = way * PIECES + n
        return remote(
            weights.at[0, pl.ds(lo, rows)], relay.at[i], s_send.at[i], s_recv.at[i], (right, left)[way]
        )

    def relay_copy(way, n):
        lo = way * 384 + n * rows
        i = way * PIECES + n
        return remote(
            relay.at[i], weights.at[1, pl.ds(lo, rows)], r_send.at[i], r_recv.at[i], (right, left)[way]
        )

    def block_copy(k):
        if k == 7:
            return remote(blocks.at[5, 0], blocks.at[7, 0], a_send.at[7], a_recv.at[7], up)
        if k == 8:
            return remote(blocks.at[6, 1], blocks.at[7, 1], a_send.at[8], a_recv.at[8], down)
        source = max(k - 2, 0)
        return remote(blocks.at[source], blocks.at[k], a_send.at[k], a_recv.at[k], up if k % 2 else down)

    block_copy(1).start()
    block_copy(2).start()
    for n in range(PIECES):
        for way in range(2):
            swap_copy(way, n).start()

    def core_copy(i):
        return remote(core_out.at[i], core_in.at[i], core_send.at[i], core_recv.at[i], core_peer)

    def y_copy(i, d):
        to = (y + d) % 4
        return remote(y_out.at[i, to], y_in.at[i, d - 1], y_send.at[i, d - 1], y_recv.at[i, d - 1], at(y=to))

    def x_copy(i):
        return remote(x_out.at[i], x_in.at[i], x_send.at[i], x_recv.at[i], xl_peer)

    def fin_slot(i):
        g = i // 8
        return (xh + g - 2 * xh * g) * 8 + z

    def fin_copy(i, to_z):
        s = fin_slot(i)
        return remote(fin_out.at[i], fin_in.at[s], f_send.at[i], f_recv.at[s], at(z=to_z))

    def block_z(k):
        half = (k + 1) // 2
        return lax.rem(z + 8 + half - 2 * half * (k % 2), 8)

    def slot(i, carry):
        for k in range(1, 8):
            @pl.when(i == k)
            def _():
                block_copy(k).wait_recv()
                if k == 7:
                    block_copy(8).wait_recv()
                if k <= 4:
                    block_copy(k + 2).start()
                elif k <= 6:
                    block_copy(k + 2).start()
                if 1 <= k <= PIECES:
                    for way in range(2):
                        swap_copy(way, k - 1).wait_recv()
                        relay_copy(way, k - 1).start()

        @pl.when(i == 8)
        def _():
            for n in range(PIECES):
                for way in range(2):
                    relay_copy(way, n).wait_recv()

        @pl.when(i < UNITS)
        def _():
            k, g = i % 8, i // 8
            theirs = contract(blocks[k, 1 - c].reshape(128, 768), weights[g])
            core_out[i] = theirs.astype(jnp.bfloat16).reshape(4, 32, 768)
            core_copy(i).start()
            own[i] = contract(blocks[k, c].reshape(128, 768), weights[g]).reshape(4, 32, 768)

        j = i - LAG

        @pl.when(jnp.logical_and(j >= 0, j < UNITS))
        def _():
            core_copy(j).wait_recv()
            total = own[j] + core_in[j].astype(jnp.float32)
            own[j] = total
            y_out[j] = total.astype(jnp.bfloat16)
            for d in (2, 1, 3):
                y_copy(j, d).start()

        m = i - 2 * LAG

        @pl.when(jnp.logical_and(m >= 0, m < UNITS))
        def _():
            for d in (1, 2, 3):
                y_copy(m, d).wait_recv()
            got = y_in[m].astype(jnp.float32)
            total = ((own[m, y] + got[0]) + (got[1] + got[2])).reshape(2, 16, 768)
            pair[m] = total
            x_out[m] = pair[m, 1 - xl].astype(jnp.bfloat16)
            x_copy(m).start()

        n = i - 3 * LAG

        @pl.when(jnp.logical_and(n >= 0, n < UNITS))
        def _():
            x_copy(n).wait_recv()
            done = (pair[n, xl] + x_in[n].astype(jnp.float32)).astype(jnp.bfloat16)
            k = n % 8

            @pl.when(k == 0)
            def _():
                fin_in[fin_slot(n)] = done

            @pl.when(k != 0)
            def _():
                fin_out[n] = done
                fin_copy(n, block_z(k)).start()

        return carry

    lax.fori_loop(0, UNITS + 3 * LAG, slot, 0)

    def take(s, carry):
        @pl.when(s % 8 != z)
        def _():
            remote(fin_out.at[0], fin_in.at[s], f_send.at[0], f_recv.at[s], core_peer).wait_recv()
        out_ref[:, pl.ds(pl.multiple_of(s * 768, 128), 768)] = fin_in[s].astype(out_ref.dtype)
        return carry

    lax.fori_loop(0, 16, take, 0)

    for k in range(1, 9):
        block_copy(k).wait_send()
    for n in range(PIECES):
        for way in range(2):
            swap_copy(way, n).wait_send()
            relay_copy(way, n).wait_send()

    def drain(i, carry):
        core_copy(i).wait_send()
        for d in (1, 2, 3):
            y_copy(i, d).wait_send()
        x_copy(i).wait_send()

        @pl.when(i % 8 != 0)
        def _():
            fin_copy(i, block_z(i % 8)).wait_send()
        return carry

    lax.fori_loop(0, UNITS, drain, 0)


def short_call(residual_grad, shortcut):
    bf, f32, dma = jnp.bfloat16, jnp.float32, pltpu.SemaphoreType.DMA
    v = pltpu.VMEM
    return pl.pallas_call(
        short_kernel,
        out_shape=jax.ShapeDtypeStruct((16, 12288), f32),
        in_specs=[pl.BlockSpec(memory_space=pl.ANY)] * 2,
        out_specs=pl.BlockSpec(memory_space=pltpu.VMEM),
        scratch_shapes=[
            v((8, 2, 8, 16, 768), bf), v((2, 768, 768), bf), v((2 * PIECES, 384 // PIECES, 768), bf),
            v((UNITS, 4, 32, 768), bf), v((UNITS, 4, 32, 768), bf), v((UNITS, 4, 32, 768), f32),
            v((UNITS, 4, 32, 768), bf), v((UNITS, 3, 32, 768), bf),
            v((UNITS, 2, 16, 768), f32), v((UNITS, 16, 768), bf), v((UNITS, 16, 768), bf),
            v((UNITS, 16, 768), bf), v((16, 16, 768), bf),
            dma((3,)), dma((9,)), dma((9,)),
            dma((2 * PIECES,)), dma((2 * PIECES,)), dma((2 * PIECES,)), dma((2 * PIECES,)),
            dma((UNITS,)), dma((UNITS,)), dma((UNITS, 3)), dma((UNITS, 3)),
            dma((UNITS,)), dma((UNITS,)), dma((UNITS,)), dma((16,)),
        ],
        compiler_params=pltpu.CompilerParams(
            collective_id=0, has_side_effects=True, vmem_limit_bytes=56 * 1024 * 1024
        ),
        cost_estimate=pl.CostEstimate(flops=4_900_000_000, bytes_accessed=4_000_000, transcendentals=0),
    )(residual_grad.reshape(8, 2, 16, 768), shortcut)
epsilon = 1e-05
adapter_scale = 0.25
HIGH = lax.Precision.HIGHEST


def shards(hidden_in, residual_grad, key_value_gradient, shortcut, key_value_weight, adapter_down_matrix, adapter_up):
    q = lax.axis_index("tensor")
    features = adapter_down_matrix.shape[0]
    inputs = hidden_in.astype(jnp.float32)
    down_rows = lax.dynamic_slice_in_dim(adapter_down_matrix, q * 768, 768, 0)
    sums = jnp.concatenate(
        [
            jnp.dot(inputs, down_rows, precision=HIGH),
            jnp.broadcast_to(jnp.sum(inputs * inputs, axis=1, keepdims=True), (256, 64)),
        ],
        axis=1,
    )
    swapped = lax.ppermute(key_value_weight, ("dp", "tensor"), [(a * 16 + b, b * 16 + a) for a in range(16) for b in range(16)])
    kv_rows = lax.all_gather(swapped, "dp", axis=1, tiled=True)
    kv_all = lax.all_gather(key_value_gradient, "tensor", axis=1, tiled=True)
    sums = lax.psum(sums, "tensor")
    scale = lax.rsqrt(sums[:, 64:65] / features + epsilon)
    low = scale * sums[:, :64]
    back = jnp.dot(kv_all.astype(jnp.float32), adapter_up.T, precision=HIGH)
    normed = inputs * scale
    down_part = adapter_scale * jnp.dot(normed.T, back, precision=HIGH)
    up_part = adapter_scale * jnp.dot(key_value_gradient.astype(jnp.float32).T, low, precision=HIGH)
    shared = lax.psum_scatter(jnp.concatenate([down_part, up_part], axis=0), "dp", scatter_dimension=0, tiled=True)
    grads = lax.all_gather(shared, ("tensor", "dp"), axis=0, tiled=True).reshape(16, 896, 64)
    down_gradient = grads[:, :768].reshape(features, 64)
    up_gradient = grads[:, 768:].reshape(2048, 64).T
    grad_norm = contract(kv_all, kv_rows) + adapter_scale * jnp.dot(back, down_rows.T, precision=HIGH)
    inner = lax.psum(jnp.sum(grad_norm * normed, axis=1, keepdims=True), "tensor") / features
    rest = (scale * (grad_norm - normed * inner)).astype(jnp.bfloat16)
    rest = lax.all_to_all(rest, "tensor", split_axis=0, concat_axis=1, tiled=True)
    short = short_call(residual_grad, shortcut)
    return ((short + rest.astype(jnp.float32)).astype(jnp.bfloat16), down_gradient, up_gradient)


def solution(mesh):
    split = P("dp", "tensor")
    return jax.shard_map(
        shards, mesh=mesh, in_specs=(split,) * 5 + (P(), P()),
        out_specs=(P(("dp", "tensor"), None), P(), P()), check_vma=False,
    )
```

time: 938 us -> 1180 us (1.26)
  waiting for transfers between devices: 825 us -> 1000 us
  Pallas kernels: 0 us -> 75.4 us
  matrix products: 31.4 us -> 13.2 us
  local copies, waits for them, and re-layouts: 8.45 us -> 22.8 us
  other arithmetic: 20.5 us -> 7.15 us
    all_gather x2 -> x3, waiting for transfers between devices: 335 us -> 735 us  [the longest x1 603 us: shards(): lax.all_gather(shared, ('tensor', 'dp'), axis=0, tiled=True)]
    reduce_scatter x1 -> x0, waiting for transfers between devices: 223 us -> none  [shards(): lax.psum_scatter(jnp.concatenate([shortcut_term, norm_term], axis=1), 'te...]
    psum x2 -> x1, waiting for transfers between devices: 266 us -> 124 us  [shards(): sums = lax.psum(sums, 'tensor')]
    unnamed x5 -> x6, waiting for transfers between devices: 1.43 us -> 139 us
    pallas_call x0 -> x1, Pallas kernels: none -> 75.4 us  [short_call(): pl.pallas_call(short_kernel, out_shape=jax.ShapeDtypeStruct((16, 12288),...]
    dot_general x7 -> x6, matrix products: 31.4 us -> 13.2 us  [the longest x1 4.3 us: contract(): lax.dot_general(a, b, (((1,), (1,)), ((), ())), preferred_element_type=jn...]
    concatenate x1 -> x2, other arithmetic: 18.3 us -> 2.13 us  [the longest x1 1.46 us: shards(): jnp.concatenate([down_part, up_part], axis=0)]
  transfers between devices with their start and end apart: 6 -> 7, of which waited for: 4 -> 6; matrix products, arithmetic and copies ran while one was open for 6% -> 1% of each run, Pallas kernels for 0% -> 6%
where the time goes in v1:
time: 1180 us; the launch traced here: 1170 us
  waiting for transfers between devices  1000 us (85%)
  Pallas kernels  75.4 us (6%)
  blocking collectives  30.2 us (3%)
  local copies, waits for them, and re-layouts  22.8 us (2%)
  between operations  14.6 us (1%)
  matrix products  13.2 us (1%)
    all_gather x1, waiting for transfers between devices, shards(): lax.all_gather(shared, ('tensor', 'dp'), axis=0, tiled=True)  603 us
    unnamed x6, waiting for transfers between devices  139 us
    psum x1, waiting for transfers between devices, shards(): sums = lax.psum(sums, 'tensor')  124 us
    all_gather x1, waiting for transfers between devices, shards(): kv_rows = lax.all_gather(swapped, 'dp', axis=1, tiled=True)  94.8 us
    pallas_call x1, Pallas kernels, short_call(): pl.pallas_call(short_kernel, out_shape=jax.ShapeDtypeStruct((16, 12288),...  75.4 us
    all_gather x1, waiting for transfers between devices, shards(): kv_all = lax.all_gather(key_value_gradient, 'tensor', axis=1, tiled=True)  37.3 us
    psum x1, blocking collectives, shards(): lax.psum(jnp.sum(grad_norm * normed, axis=1, keepdims=True), 'tensor')  30.2 us
  transfers between devices with their start and end apart: 7, of which 6 were waited for; matrix products, arithmetic and copies ran while one was open for 1% of the time, Pallas kernels for 6%

profile of v1, /device:TPU:1, one launch (start us, length us, event | category | flops | bytes accessed | tf_op | source)
XLA Modules:
  0.0 1172.4 jit_solution(608949017844534010)
XLA Ops:
  7.2 0.0 copy-start
  7.2 0.0 copy-start.4
  7.2 0.0 copy-start.1
  7.2 0.0 all-reduce.4.cloned.1.call-start
  7.3 1.3 fusion.7
  8.6 0.7 copy-done
  9.3 1.5 convolution_bitcast_fusion
  10.8 0.7 pad_maximum_fusion.1
  11.5 0.0 all-reduce.4.cloned.1.call-update
  11.5 0.0 all-gather.4.cloned.1.call-start
  11.6 0.7 all-gather.4.cloned.1.call-update
  12.3 0.0 all-reduce.6.cloned.1.call-start
  12.3 123.9 %all-reduce.4.cloned.1.call-done = f32[256,128]{0,1:T(8,128)} async-done(((f32[256,128]{0,1:T(8,128)}), f32[256,128]{0,1:T(8,128)}) %all-reduce.4.cloned.1.call-update) | async-done | bytes 131088 | tf_op jit(solution)/shard_map/psum | solution.py:260
  136.2 0.7 fusion.13
  136.9 1.7 fusion
  138.5 37.3 %all-gather.4.cloned.1.call-done = bf16[256,2048]{1,0:T(8,128)(2,1)} async-done(((bf16[256,128]{1,0:T(8,128)(2,1)}), bf16[256,2048]{1,0:T(8,128)(2,1)}) %all-gather.4.cloned.1.call-update) | async-done | bytes 1048592 | tf_op jit(solution)/shard_map/all_gather | solution.py:259
  175.8 2.4 fusion.16
  178.2 0.0 copy-start.3
  178.3 0.6 copy-done.3
  178.9 0.0 copy-done.1
  178.9 0.7 convolution_multiply_fusion.1
  179.6 1.5 pad_maximum_fusion
  181.1 0.0 all-reduce.6.cloned.1.call-update
  181.1 0.0 all-gather.6.cloned.1.call-start
  181.2 3.3 collective-permute-start
  184.5 4.2 collective-permute-done
  188.7 0.0 all-gather.6.cloned.1.call-update
  188.7 0.0 all-gather.8.cloned.1.call-start
  188.8 0.0 copy-done.4
  188.8 0.6 dynamic-slice
  190.0 137.9 %all-reduce.6.cloned.1.call-done = f32[896,64]{0,1:T(8,128)} async-done(((f32[896,64]{0,1:T(8,128)}), f32[896,64]{0,1:T(8,128)}) %all-reduce.6.cloned.1.call-update) | async-done | bytes 229392
  327.9 1.5 constant_dynamic-slice_fusion
  329.5 1.4 copy.12
  330.9 0.0 all-gather.8.cloned.1.call-update
  330.9 2.6 convolution_multiply_fusion
  333.5 94.8 %all-gather.6.cloned.1.call-done = bf16[768,2048]{1,0:T(8,128)(2,1)} async-done(((bf16[768,128]{1,0:T(8,128)(2,1)}), bf16[768,2048]{1,0:T(8,128)(2,1)}) %all-gather.6.cloned.1.call-update) | async-done | bytes 3145744 | tf_op jit(solution)/shard_map/all_gather | solution.py:258
  428.3 4.3 fusion.3
  432.6 30.2 %psum.15 = f32[256,1]{0,1:T(1,128)S(1)} all-reduce(f32[256,1]{0,1:T(1,128)S(1)} %bitcast.40), channel_id=1, replica_groups=mesh['dp'=16,'tensor'=16] {'tensor'}, use_global_device_ids=true, to_apply=%region_3.0 | all-reduce | flops 256 | bytes 2048 | tf_op jit(solution)/shard_map/psum | solution.py:272
  462.8 2.1 fusion.6
  464.9 4.1 all-to-all-start
  469.0 75.4 %shard_map.94 = f32[16,12288]{1,0:T(8,128)} custom-call(bf16[8,2,16,768]{3,2,1,0:T(8,128)(2,1)} %bitcast.41, bf16[768,768]{1,0:T(8,128)(2,1)} %short_ref.1), custom_call_target="tpu_custom_call" | custom-call | flops 4899999744 | bytes 4000000 | tf_op jit(solution)/shard_map/pallas_call | solution.py:219
  544.4 0.0 all-to-all-done
  544.4 0.0 copy-start.2
  544.4 0.1 convert_bitcast_fusion
  544.5 0.1 copy.19
  544.6 1.0 copy-done.2
  545.6 0.8 add_convert_fusion
  546.4 602.7 %all-gather.8.cloned.1.call-done = f32[14336,64]{1,0:T(8,128)} async-done(((f32[56,64]{1,0:T(8,128)}), f32[14336,64]{1,0:T(8,128)}) %all-gather.8.cloned.1.call-update) | async-done | bytes 3670032 | tf_op jit(solution)/shard_map/all_gather | solution.py:268
  1149.1 2.3 slice.19
  1151.4 6.1 slice.18
  1157.5 6.1 copy.15
  1163.6 2.3 copy.16
  (2 shorter events, 0.0 us)
Async XLA Ops:
  7.2 2.1 copy-start
  7.2 181.6 %copy-start.4 = (u32[256]{0:T(256)S(1)}, u32[256]{0:T(256)}, u32[]{:S(2)}) copy-start(u32[256]{0:T(256)} %constant.24) | copy-start | bytes 3076
  7.2 171.7 %copy-start.1 = (bf16[256,768]{1,0:T(8,128)(2,1)S(1)}, bf16[256,768]{1,0:T(8,128)(2,1)}, u32[]{:S(2)}) copy-start(bf16[256,768]{1,0:T(8,128)(2,1)} %param.7) | copy-start | bytes 1179652
  7.2 129.0 %all-reduce.4.cloned.1.call-start = ((), (), s32[]{:S(2)}) async-start(), calls=%async_computation.1 | async-start | bytes 262144 | tf_op jit(solution)/shard_map/psum | solution.py:260
  11.5 164.3 %all-gather.4.cloned.1.call-start = ((), (), s32[]{:S(2)}) async-start(), calls=%async_computation.2 | async-start | bytes 1114112 | tf_op jit(solution)/shard_map/all_gather | solution.py:259
  12.3 315.7 %all-reduce.6.cloned.1.call-start = ((), (), s32[]{:S(2)}) async-start(), calls=%async_computation.5 | async-start | bytes 458752
  178.2 0.6 copy-start.3
  181.1 247.2 %all-gather.6.cloned.1.call-start = ((), (), s32[]{:S(2)}) async-start(), calls=%async_computation.3 | async-start | bytes 3342336 | tf_op jit(solution)/shard_map/all_gather | solution.py:258
  181.2 7.5 collective-permute-start
  188.7 960.4 %all-gather.8.cloned.1.call-start = ((), (), s32[]{:S(2)}) async-start(), calls=%async_computation.4 | async-start | bytes 7368704 | tf_op jit(solution)/shard_map/all_gather | solution.py:268
  464.9 79.5 %all-to-all-start = ((bf16[16,16,768]{2,1,0:T(8,128)(2,1)}), bf16[16,16,768]{2,1,0:T(8,128)(2,1)S(1)}, u32[]{:S(2)}, u32[]{:S(2)}) async-start(bf16[16,16,768]{2,1,0:T(8,128)(2,1)} %bitcast.33), calls=%async_computation | async-start | bytes 786432 | tf_op jit(solution)/shard_map/all_to_all | solution.py:274
  544.4 1.1 copy-start.2
Sparse Core Ops, SparseCore 0:
  11.6 124.4 all-reduce.3
  138.1 37.7 all-gather.3
  181.2 146.6 all-reduce.5
  330.3 97.9 all-gather.5
  430.0 719.0 all-gather.7

commit v2 on v1

--- a/solution.py
+++ b/solution.py
@@ -9,6 +9,8 @@
 UNITS = 16
 LAG = 2
 PIECES = 4
+epsilon = 1e-05
+adapter_scale = 0.25
 
 
 def place(xh, z, y, xl, c):
@@ -19,11 +21,25 @@
     return lax.dot_general(a, b, (((1,), (1,)), ((), ())), preferred_element_type=jnp.float32)
 
 
-def short_kernel(
-    grad_ref, short_ref, out_ref,
+def contract_first(a, b):
+    return lax.dot_general(a, b, (((0,), (0,)), ((), ())), preferred_element_type=jnp.float32)
+
+
+def split(value):
+    hi = value.astype(jnp.bfloat16)
+    return hi, (value - hi.astype(jnp.float32)).astype(jnp.bfloat16)
+
+
+def whole_kernel(
+    grad_ref, short_ref, hidden_ref, kv_ref, kvw_ref, down_ref, up_ref,
+    out_ref, down_out, up_out,
     blocks, weights, relay, core_out, core_in, own, y_out, y_in, pair, x_out, x_in, fin_out, fin_in,
     load_sem, a_send, a_recv, s_send, s_recv, r_send, r_recv,
     core_send, core_recv, y_send, y_recv, x_send, x_recv, f_send, f_recv,
+    hidden, hidden_in, kv_all, w_ring, down_rows, up_rows, sums_out, sums_in, sums_all, back_keep,
+    norm_sum, norm_out, norm_in, g_out, g_in, g_all,
+    h_send, h_recv, k_send, k_recv, su_send, su_recv, sa_send, sa_recv, n_send, n_recv,
+    gs_send, gs_recv, gd_send, gd_recv, gt_send, gt_recv, gc_send, gc_recv, t_sem, w_send, w_recv,
 ):
     p, q = lax.axis_index("dp"), lax.axis_index("tensor")
     xh, z = p // 8, p % 8
@@ -41,16 +57,39 @@
 
     loads = [pltpu.make_async_copy(grad_ref.at[:, h], blocks.at[0, h], load_sem.at[h]) for h in range(2)]
     loads.append(pltpu.make_async_copy(short_ref, weights.at[0], load_sem.at[2]))
+    loads.append(pltpu.make_async_copy(hidden_ref, hidden, load_sem.at[3]))
+    loads.append(pltpu.make_async_copy(hidden_ref.at[q], hidden_in.at[q], load_sem.at[4]))
+    loads.append(pltpu.make_async_copy(kv_ref, kv_all.at[q], load_sem.at[5]))
+    loads.append(
+        pltpu.make_async_copy(down_ref.at[pl.ds(pl.multiple_of(q * 768, 768), 768)], down_rows, load_sem.at[6])
+    )
+    loads.append(pltpu.make_async_copy(up_ref, up_rows, load_sem.at[7]))
     for l in loads:
         l.start()
 
     barrier = pltpu.get_barrier_semaphore()
-    peers = [core_peer, right, left] + [at(y=(y + d) % 4) for d in (1, 2, 3)] + [at(z=(z + d) % 8) for d in range(1, 8)]
-    for peer in peers:
-        pl.semaphore_signal(barrier, inc=1, device_id=peer, device_id_type=MESH)
+    def greet(d, carry):
+        pl.semaphore_signal(barrier, inc=1, device_id={"dp": p, "tensor": (q + d) % 16}, device_id_type=MESH)
+        pl.semaphore_signal(barrier, inc=1, device_id={"dp": (p + d) % 16, "tensor": q}, device_id_type=MESH)
+        return carry
+
+    lax.fori_loop(1, 16, greet, 0)
+    pl.semaphore_signal(barrier, inc=1, device_id=at(xh=1 - xh, xl=1 - xl), device_id_type=MESH)
+
+    @pl.when(p != q)
+    def _():
+        pl.semaphore_signal(barrier, inc=1, device_id={"dp": q, "tensor": p}, device_id_type=MESH)
+
     for l in loads:
         l.wait()
-    pl.semaphore_wait(barrier, len(peers))
+
+    @pl.when(p != q)
+    def _():
+        pl.semaphore_wait(barrier, 32)
+
+    @pl.when(p == q)
+    def _():
+        pl.semaphore_wait(barrier, 31)
 
     def remote(src, dst, send, recv, to):
         return pltpu.make_async_remote_copy(
@@ -87,6 +126,152 @@
         for way in range(2):
             swap_copy(way, n).start()
 
+    def tensor_copy(source, target, send, recv, d):
+        return remote(source, target, send.at[d - 1], recv.at[d - 1], {"dp": p, "tensor": (q + d) % 16})
+
+    def dp_copy(source, target, send, recv, d):
+        return remote(source, target, send.at[d - 1], recv.at[d - 1], {"dp": (p + d) % 16, "tensor": q})
+
+    def each(body, count=16):
+        def step(d, carry):
+            body(d)
+            return carry
+        lax.fori_loop(1, count, step, 0)
+
+    def turn_copy():
+        return remote(kvw_ref, w_ring.at[0, q // 8], t_sem.at[0], t_sem.at[1], {"dp": q, "tensor": p})
+
+    def turned():
+        return remote(kvw_ref, w_ring.at[0, xh], t_sem.at[0], t_sem.at[1], {"dp": q, "tensor": p})
+
+    def turn_local():
+        return pltpu.make_async_copy(kvw_ref, w_ring.at[0, xh], t_sem.at[0])
+
+    def half_copy(which):
+        return remote(w_ring.at[0, which], w_ring.at[0, which], t_sem.at[2], t_sem.at[3], at(xh=1 - xh))
+
+    def w_copy(k):
+        if k == 7:
+            return remote(w_ring.at[5, 0], w_ring.at[7, 0], w_send.at[7], w_recv.at[7], up)
+        if k == 8:
+            return remote(w_ring.at[6, 1], w_ring.at[7, 1], w_send.at[8], w_recv.at[8], down)
+        return remote(w_ring.at[max(k - 2, 0)], w_ring.at[k], w_send.at[k], w_recv.at[k], up if k % 2 else down)
+
+    @pl.when(p != q)
+    def _():
+        turn_copy().start()
+
+    @pl.when(p == q)
+    def _():
+        turn_local().start()
+
+    down_hi, down_lo = split(down_rows[...])
+    local = hidden[...].reshape(256, 768)
+    low = jnp.dot(local, jnp.concatenate([down_hi, down_lo], axis=1), preferred_element_type=jnp.float32)
+    wide = local.astype(jnp.float32)
+    squares = jnp.sum(wide * wide, axis=1, keepdims=True)
+    sums = jnp.concatenate([low[:, :64] + low[:, 64:], jnp.broadcast_to(squares, (256, 64))], axis=1)
+    sums_out[...] = sums.reshape(16, 16, 128)
+    each(lambda d: tensor_copy(sums_out.at[(q + d) % 16], sums_in.at[q], su_send, su_recv, d).start())
+    sums_in[q] = sums_out[q]
+    each(lambda d: tensor_copy(kv_ref, kv_all.at[q], k_send, k_recv, d).start())
+    each(lambda d: tensor_copy(hidden_ref.at[(q + d) % 16], hidden_in.at[q], h_send, h_recv, d).start())
+
+    def sums_reduce():
+        each(lambda d: tensor_copy(sums_out.at[0], sums_in.at[(q + 16 - d) % 16], su_send, su_recv, d).wait_recv())
+        sums_all[q] = jnp.sum(sums_in[...], axis=0)
+        each(lambda d: tensor_copy(sums_all.at[q], sums_all.at[q], sa_send, sa_recv, d).start())
+
+    def adapter_parts():
+        each(lambda d: tensor_copy(sums_out.at[0], sums_all.at[(q + 16 - d) % 16], sa_send, sa_recv, d).wait_recv())
+        each(lambda d: tensor_copy(kv_ref, kv_all.at[(q + 16 - d) % 16], k_send, k_recv, d).wait_recv())
+
+        def add(s, total):
+            hi, lo = split(up_rows[:, pl.ds(pl.multiple_of(s * 128, 128), 128)])
+            return total + contract(kv_all[s], jnp.concatenate([hi, lo], axis=0))
+
+        both = lax.fori_loop(0, 16, add, jnp.zeros((256, 128), jnp.float32))
+        back = both[:, :64] + both[:, 64:]
+        back_keep[...] = back
+        reduced = sums_all[...].reshape(256, 128)
+        scale = lax.rsqrt(reduced[:, 64:65] / 12288 + epsilon)
+        low = jnp.concatenate(split(scale * reduced[:, :64]), axis=1)
+        upper = contract_first(low, kv_all[q])
+        g_out[...] = jnp.zeros_like(g_out)
+        g_out[0:8, 24:32] = (adapter_scale * (upper[:64] + upper[64:])).reshape(8, 8, 128)
+        scaled = jnp.concatenate(split(scale * back), axis=1)
+        lower = contract_first(hidden[...].reshape(256, 768), scaled)
+        lower = adapter_scale * (lower[:, :64] + lower[:, 64:])
+        g_out[:, 0:24] = jnp.concatenate([lower[:384], lower[384:]], axis=1).reshape(16, 24, 128)
+        each(lambda d: dp_copy(g_out.at[(p + d) % 16], g_in.at[p], gs_send, gs_recv, d).start())
+        g_in[p] = g_out[p]
+
+    def grads_reduce():
+        each(lambda d: dp_copy(g_out.at[0], g_in.at[(p + 16 - d) % 16], gs_send, gs_recv, d).wait_recv())
+        g_all[q, p] = jnp.sum(g_in[...], axis=0).astype(jnp.bfloat16)
+        each(lambda d: dp_copy(g_all.at[q, p], g_all.at[q, p], gd_send, gd_recv, d).start())
+
+    def chips_copy(s, e):
+        return remote(
+            g_all.at[s], g_all.at[s], gt_send.at[e - 1], gt_recv.at[e - 1], {"dp": p, "tensor": (q + 2 * e) % 16}
+        )
+
+    def other_core_copy(s, e):
+        return remote(g_all.at[s], g_all.at[s], gc_send.at[e], gc_recv.at[e], core_peer)
+
+    def grads_spread():
+        each(lambda d: dp_copy(g_all.at[0, 0], g_all.at[q, (p + 16 - d) % 16], gd_send, gd_recv, d).wait_recv())
+        each(lambda e: chips_copy(q, e).start(), 8)
+        other_core_copy(q, 0).start()
+
+    def grads_forward():
+        def body(e):
+            s = (q + 16 - 2 * e) % 16
+            chips_copy(s, e).wait_recv()
+            other_core_copy(s, e).start()
+        each(body, 8)
+
+    def norm_add(k, first=False):
+        z_from = block_z(k)
+        term = contract(kv_all[z_from], w_ring[k, 0]) + contract(kv_all[8 + z_from], w_ring[k, 1])
+        norm_sum[...] = term if first else norm_sum[...] + term
+
+    def norm_begin():
+        half_copy(1 - xh).wait_recv()
+        w_copy(1).start()
+        w_copy(2).start()
+        norm_add(0, True)
+        back_hi, back_lo = split(back_keep[...])
+        down_hi, down_lo = split(down_rows[...])
+        extra = contract(
+            jnp.concatenate([back_hi, back_lo], axis=1), jnp.concatenate([down_hi, down_hi], axis=1)
+        ) + contract(back_hi, down_lo)
+        norm_sum[...] += adapter_scale * extra
+
+    def norm_hop(first, second):
+        for k in (first, second):
+            w_copy(k).wait_recv()
+            if k < 7:
+                w_copy(k + 2).start()
+        for k in ((first, second) if first < 7 else (7,)):
+            norm_add(k)
+
+    def norm_send():
+        norm_out[...] = norm_sum[...].astype(jnp.bfloat16).reshape(16, 16, 768)
+        each(lambda d: tensor_copy(norm_out.at[(q + d) % 16], norm_in.at[q], n_send, n_recv, d).start())
+        norm_in[q] = norm_out[q]
+
+    def turn_done():
+        @pl.when(p != q)
+        def _():
+            turned().wait_recv()
+
+        @pl.when(p == q)
+        def _():
+            turn_local().wait()
+
+        half_copy(xh).start()
+
     def core_copy(i):
         return remote(core_out.at[i], core_in.at[i], core_send.at[i], core_recv.at[i], core_peer)
 
@@ -108,6 +293,12 @@
     def block_z(k):
         half = (k + 1) // 2
         return lax.rem(z + 8 + half - 2 * half * (k % 2), 8)
+
+    plan = {
+        2: [turn_done], 3: [sums_reduce], 5: [adapter_parts], 7: [grads_reduce, norm_begin], 9: [grads_spread],
+        10: [lambda: norm_hop(1, 2)], 13: [lambda: norm_hop(3, 4)], 14: [grads_forward],
+        16: [lambda: norm_hop(5, 6)], 19: [lambda: norm_hop(7, 8), norm_send],
+    }
 
     def slot(i, carry):
         for k in range(1, 8):
@@ -139,6 +330,12 @@
             core_copy(i).start()
             own[i] = contract(blocks[k, c].reshape(128, 768), weights[g]).reshape(4, 32, 768)
 
+        for when, acts in plan.items():
+            @pl.when(i == when)
+            def _(acts=acts):
+                for act in acts:
+                    act()
+
         j = i - LAG
 
         @pl.when(jnp.logical_and(j >= 0, j < UNITS))
@@ -183,11 +380,37 @@
 
     lax.fori_loop(0, UNITS + 3 * LAG, slot, 0)
 
+    each(lambda e: other_core_copy((q + 1 - 2 * c + 16 - 2 * e) % 16, e).wait_recv(), 8)
+    other_core_copy(q + 1 - 2 * c, 0).wait_recv()
+
+    def unpack(s, carry):
+        packed = g_all[s].astype(jnp.float32)
+        lower = packed[:, :24].reshape(384, 128)
+        first = pl.multiple_of(s * 768, 128)
+        down_out[pl.ds(first, 384)] = lower[:, :64].astype(down_out.dtype)
+        down_out[pl.ds(first + 384, 384)] = lower[:, 64:].astype(down_out.dtype)
+        up_out[:, pl.ds(pl.multiple_of(s * 128, 128), 128)] = packed[:8, 24:].reshape(64, 128).astype(up_out.dtype)
+        return carry
+
+    lax.fori_loop(0, 16, unpack, 0)
+
+    each(lambda d: tensor_copy(kv_ref, hidden_in.at[(q + 16 - d) % 16], h_send, h_recv, d).wait_recv())
+    each(lambda d: tensor_copy(norm_out.at[0], norm_in.at[(q + 16 - d) % 16], n_send, n_recv, d).wait_recv())
+    my_scale = lax.rsqrt(sums_all[q][:, 64:65] / 12288 + epsilon)
+
+    def dots(s, total):
+        return total + hidden_in[s].astype(jnp.float32) * norm_in[s].astype(jnp.float32)
+
+    products = lax.fori_loop(0, 16, dots, jnp.zeros((16, 768), jnp.float32))
+    inner = jnp.sum(products, axis=1, keepdims=True) * my_scale / 12288
+
     def take(s, carry):
         @pl.when(s % 8 != z)
         def _():
             remote(fin_out.at[0], fin_in.at[s], f_send.at[0], f_recv.at[s], core_peer).wait_recv()
-        out_ref[:, pl.ds(pl.multiple_of(s * 768, 128), 768)] = fin_in[s].astype(out_ref.dtype)
+        normed = hidden_in[s].astype(jnp.float32) * my_scale
+        done = fin_in[s].astype(jnp.float32) + my_scale * (norm_in[s].astype(jnp.float32) - normed * inner)
+        out_ref[:, pl.ds(pl.multiple_of(s * 768, 128), 768)] = done.astype(out_ref.dtype)
         return carry
 
     lax.fori_loop(0, 16, take, 0)
@@ -211,74 +434,77 @@
         return carry
 
     lax.fori_loop(0, UNITS, drain, 0)
-
-
-def short_call(residual_grad, shortcut):
+    for k in range(1, 9):
+        w_copy(k).wait_send()
+    half_copy(xh).wait_send()
+
+    @pl.when(p != q)
+    def _():
+        turn_copy().wait_send()
+
+    def drain_all(d):
+        tensor_copy(sums_out.at[(q + d) % 16], sums_in.at[q], su_send, su_recv, d).wait_send()
+        tensor_copy(sums_all.at[q], sums_all.at[q], sa_send, sa_recv, d).wait_send()
+        tensor_copy(kv_ref, kv_all.at[q], k_send, k_recv, d).wait_send()
+        tensor_copy(hidden_ref.at[(q + d) % 16], hidden_in.at[q], h_send, h_recv, d).wait_send()
+        tensor_copy(norm_out.at[(q + d) % 16], norm_in.at[q], n_send, n_recv, d).wait_send()
+        dp_copy(g_out.at[(p + d) % 16], g_in.at[p], gs_send, gs_recv, d).wait_send()
+        dp_copy(g_all.at[q, p], g_all.at[q, p], gd_send, gd_recv, d).wait_send()
+
+    each(drain_all)
+    other_core_copy(q, 0).wait_send()
+
+    def drain_grads(e):
+        chips_copy(q, e).wait_send()
+        other_core_copy((q + 16 - 2 * e) % 16, e).wait_send()
+
+    each(drain_grads, 8)
+
+
+def shards(hidden_in, residual_grad, key_value_gradient, shortcut, key_value_weight, adapter_down_matrix, adapter_up):
     bf, f32, dma = jnp.bfloat16, jnp.float32, pltpu.SemaphoreType.DMA
     v = pltpu.VMEM
-    return pl.pallas_call(
-        short_kernel,
-        out_shape=jax.ShapeDtypeStruct((16, 12288), f32),
-        in_specs=[pl.BlockSpec(memory_space=pl.ANY)] * 2,
-        out_specs=pl.BlockSpec(memory_space=pltpu.VMEM),
+    result, down, up = pl.pallas_call(
+        whole_kernel,
+        out_shape=[
+            jax.ShapeDtypeStruct((16, 12288), bf),
+            jax.ShapeDtypeStruct((12288, 64), bf),
+            jax.ShapeDtypeStruct((64, 2048), bf),
+        ],
+        in_specs=[pl.BlockSpec(memory_space=pl.ANY)] * 7,
+        out_specs=[pl.BlockSpec(memory_space=pltpu.VMEM)] * 3,
         scratch_shapes=[
             v((8, 2, 8, 16, 768), bf), v((2, 768, 768), bf), v((2 * PIECES, 384 // PIECES, 768), bf),
             v((UNITS, 4, 32, 768), bf), v((UNITS, 4, 32, 768), bf), v((UNITS, 4, 32, 768), f32),
             v((UNITS, 4, 32, 768), bf), v((UNITS, 3, 32, 768), bf),
             v((UNITS, 2, 16, 768), f32), v((UNITS, 16, 768), bf), v((UNITS, 16, 768), bf),
             v((UNITS, 16, 768), bf), v((16, 16, 768), bf),
-            dma((3,)), dma((9,)), dma((9,)),
+            dma((8,)), dma((9,)), dma((9,)),
             dma((2 * PIECES,)), dma((2 * PIECES,)), dma((2 * PIECES,)), dma((2 * PIECES,)),
             dma((UNITS,)), dma((UNITS,)), dma((UNITS, 3)), dma((UNITS, 3)),
             dma((UNITS,)), dma((UNITS,)), dma((UNITS,)), dma((16,)),
+            v((16, 16, 768), bf), v((16, 16, 768), bf), v((16, 256, 128), bf), v((8, 2, 768, 128), bf),
+            v((768, 64), f32), v((64, 2048), f32), v((16, 16, 128), f32), v((16, 16, 128), f32),
+            v((16, 16, 128), f32), v((256, 64), f32),
+            v((256, 768), f32), v((16, 16, 768), bf), v((16, 16, 768), bf),
+            v((16, 32, 128), f32), v((16, 32, 128), f32), v((16, 16, 32, 128), bf),
+            *[dma((15,))] * 10, *[dma((15,))] * 4, dma((7,)), dma((7,)), dma((8,)), dma((8,)),
+            dma((4,)), dma((9,)), dma((9,)),
         ],
         compiler_params=pltpu.CompilerParams(
-            collective_id=0, has_side_effects=True, vmem_limit_bytes=56 * 1024 * 1024
+            collective_id=0, has_side_effects=True, vmem_limit_bytes=58 * 1024 * 1024
         ),
-        cost_estimate=pl.CostEstimate(flops=4_900_000_000, bytes_accessed=4_000_000, transcendentals=0),
-    )(residual_grad.reshape(8, 2, 16, 768), shortcut)
-epsilon = 1e-05
-adapter_scale = 0.25
-HIGH = lax.Precision.HIGHEST
-
-
-def shards(hidden_in, residual_grad, key_value_gradient, shortcut, key_value_weight, adapter_down_matrix, adapter_up):
-    q = lax.axis_index("tensor")
-    features = adapter_down_matrix.shape[0]
-    inputs = hidden_in.astype(jnp.float32)
-    down_rows = lax.dynamic_slice_in_dim(adapter_down_matrix, q * 768, 768, 0)
-    sums = jnp.concatenate(
-        [
-            jnp.dot(inputs, down_rows, precision=HIGH),
-            jnp.broadcast_to(jnp.sum(inputs * inputs, axis=1, keepdims=True), (256, 64)),
-        ],
-        axis=1,
+        cost_estimate=pl.CostEstimate(flops=5_900_000_000, bytes_accessed=12_000_000, transcendentals=512),
+    )(
+        residual_grad.reshape(8, 2, 16, 768), shortcut, hidden_in.reshape(16, 16, 768), key_value_gradient, key_value_weight,
+        adapter_down_matrix, adapter_up,
     )
-    swapped = lax.ppermute(key_value_weight, ("dp", "tensor"), [(a * 16 + b, b * 16 + a) for a in range(16) for b in range(16)])
-    kv_rows = lax.all_gather(swapped, "dp", axis=1, tiled=True)
-    kv_all = lax.all_gather(key_value_gradient, "tensor", axis=1, tiled=True)
-    sums = lax.psum(sums, "tensor")
-    scale = lax.rsqrt(sums[:, 64:65] / features + epsilon)
-    low = scale * sums[:, :64]
-    back = jnp.dot(kv_all.astype(jnp.float32), adapter_up.T, precision=HIGH)
-    normed = inputs * scale
-    down_part = adapter_scale * jnp.dot(normed.T, back, precision=HIGH)
-    up_part = adapter_scale * jnp.dot(key_value_gradient.astype(jnp.float32).T, low, precision=HIGH)
-    shared = lax.psum_scatter(jnp.concatenate([down_part, up_part], axis=0), "dp", scatter_dimension=0, tiled=True)
-    grads = lax.all_gather(shared, ("tensor", "dp"), axis=0, tiled=True).reshape(16, 896, 64)
-    down_gradient = grads[:, :768].reshape(features, 64)
-    up_gradient = grads[:, 768:].reshape(2048, 64).T
-    grad_norm = contract(kv_all, kv_rows) + adapter_scale * jnp.dot(back, down_rows.T, precision=HIGH)
-    inner = lax.psum(jnp.sum(grad_norm * normed, axis=1, keepdims=True), "tensor") / features
-    rest = (scale * (grad_norm - normed * inner)).astype(jnp.bfloat16)
-    rest = lax.all_to_all(rest, "tensor", split_axis=0, concat_axis=1, tiled=True)
-    short = short_call(residual_grad, shortcut)
-    return ((short + rest.astype(jnp.float32)).astype(jnp.bfloat16), down_gradient, up_gradient)
+    return result, down.astype(f32), up.astype(f32)
 
 
 def solution(mesh):
-    split = P("dp", "tensor")
+    part = P("dp", "tensor")
     return jax.shard_map(
-        shards, mesh=mesh, in_specs=(split,) * 5 + (P(), P()),
+        shards, mesh=mesh, in_specs=(part,) * 5 + (P(), P()),
         out_specs=(P(("dp", "tensor"), None), P(), P()), check_vma=False,
     )

time: 1180 us -> 160 us (0.14)
  waiting for transfers between devices: 1000 us -> 0 us
  Pallas kernels: 75.4 us -> 146 us
  blocking collectives: 30.2 us -> 0 us
  between operations: 14.6 us -> 0.64 us
  matrix products: 13.2 us -> 0 us
    all_gather x3 -> x0, waiting for transfers between devices: 735 us -> none  [the longest x1 603 us: shards(): lax.all_gather(shared, ('tensor', 'dp'), axis=0, tiled=True)]
    unnamed x6 -> x0, waiting for transfers between devices: 139 us -> none
    psum x1 -> x0, waiting for transfers between devices: 124 us -> none  [shards(): sums = lax.psum(sums, 'tensor')]
    pallas_call x1, Pallas kernels: 75.4 us -> 146 us  [shards(): pl.pallas_call(whole_kernel, out_shape=[jax.ShapeDtypeStruct((16, 12288),...]
    psum x1 -> x0, blocking collectives: 30.2 us -> none  [shards(): lax.psum(jnp.sum(grad_norm * normed, axis=1, keepdims=True), 'tensor')]
    dot_general x6 -> x0, matrix products: 13.2 us -> none  [the longest x1 4.3 us: contract(): lax.dot_general(a, b, (((1,), (1,)), ((), ())), preferred_element_type=jn...]
  transfers between devices with their start and end apart: 7 -> 0, of which waited for: 6 -> 0; matrix products, arithmetic and copies ran while one was open for 1% -> 0% of each run, Pallas kernels for 6% -> 0%
where the time goes in v2:
time: 160 us; the launch traced here: 159 us
  Pallas kernels  146 us (91%)
  local copies, waits for them, and re-layouts  11.4 us (7%)
  other arithmetic  1.78 us (1%)
    pallas_call x1, Pallas kernels, shards(): pl.pallas_call(whole_kernel, out_shape=[jax.ShapeDtypeStruct((16, 12288),...  146 us
    unnamed x5, local copies, waits for them, and re-layouts  11.4 us

profile of v2, /device:TPU:1, one launch (start us, length us, event | category | flops | bytes accessed | tf_op | source)
XLA Modules:
  0.0 159.4 jit_solution(10806540450333517083)
XLA Ops:
  0.6 5.8 %copy.10.down_ref = f32[12288,64]{1,0:T(8,128)} copy(f32[12288,64]{0,1:T(8,128)} %param.12) | data formatting | bytes 6291456 | tf_op args[5]
  6.4 145.6 %shard_map.94 = (bf16[16,12288]{1,0:T(8,128)(2,1)}, bf16[12288,64]{1,0:T(8,128)(2,1)}, bf16[64,2048]{1,0:T(8,128)(2,1)}) custom-call(bf16[8,2,16,768]{3,2,1,0:T(8,128)(2,1)} %bitcast.2, bf16[768,768]{1,0:T(8,128)(2,1)} %short_ref.1, bf16[16,16,768]{2,1,0:T(8,128)(2,1)} %bitcast.3, bf16[256,128]{1,0:T(8,128)(2,1)} %kv_ref.1, bf16[768,128]{1,0:T(8,128)(2,1)} %kvw_ref.1, ...), custom_call_target="tpu_custom_call" | custom-call | flops 5900000256 | bytes 12000000 | tf_op jit(solution)/shard_map/pallas_call | solution.py:467
  152.0 1.8 %convert_element_type.7 = f32[64,2048]{1,0:T(8,128)} convert(bf16[64,2048]{1,0:T(8,128)(2,1)} %get-tuple-element.8) | non-fusion elementwise | flops 131072 | bytes 786432 | tf_op jit(solution)/shard_map/convert_element_type | solution.py:502
  153.8 0.0 copy-start
  153.8 4.9 %copy.11 = f32[12288,64]{0,1:T(8,128)} copy(bf16[12288,64]{1,0:T(8,128)(2,1)} %get-tuple-element.7) | data formatting | bytes 4718592
  158.7 0.0 copy-done
  158.7 0.7 copy.13
Async XLA Ops:
  153.8 4.9 %copy-start = (bf16[16,12288]{1,0:T(8,128)(2,1)S(1)}, bf16[16,12288]{1,0:T(8,128)(2,1)}, u32[]{:S(2)}) copy-start(bf16[16,12288]{1,0:T(8,128)(2,1)} %get-tuple-element.15) | copy-start | bytes 1179652

commit v3 on v0

v3 whole, which is shorter than its diff:
```python
import jax
import jax.numpy as jnp
from jax import lax
from jax.experimental import pallas as pl
from jax.experimental.pallas import tpu as pltpu
from jax.sharding import PartitionSpec as P

MESH = pl.DeviceIdType.MESH
UNITS = 8
LAGS = (1, 2, 3, 4)
epsilon = 1e-05
adapter_scale = 0.25


def place(xh, z, y, xl, c):
    return {"dp": xh * 8 + z, "tensor": (y * 2 + xl) * 2 + c}


def contract(a, b):
    return lax.dot_general(a, b, (((1,), (1,)), ((), ())), preferred_element_type=jnp.float32)


def multiply(a, b):
    return jnp.dot(a, b, preferred_element_type=jnp.float32)


def contract_first(a, b):
    return lax.dot_general(a, b, (((0,), (0,)), ((), ())), preferred_element_type=jnp.float32)


def split(value):
    hi = value.astype(jnp.bfloat16)
    return hi, (value - hi.astype(jnp.float32)).astype(jnp.bfloat16)


def whole_kernel(
    grad_ref, short_ref, hidden_ref, kv_ref, kvw_ref, down_ref, up_ref,
    out_ref, down_out, up_out,
    blocks, weights, core_out, core_in, own, y_out, far_in, y_in, pair, x_out, x_in, fin_out, fin_in,
    hidden, hidden_in, kv_all, w_ring, down_rows, up_rows, sums_out, sums_in, sums_all, back_keep,
    norm_sum, norm_out, norm_in, g_out, g_in, g_all, g_rows,
    load_sem, a_send, a_recv, s_sem,
    core_send, core_recv, far_send, far_recv, near_send, near_recv, x_send, x_recv, f_sem,
    h_sem, k_sem, su_sem, sa_sem, n_sem, gs_sem, gd_sem, gt_send, gt_recv, gc_sem, t_sem, w_send, w_recv,
):
    p, q = lax.axis_index("dp"), lax.axis_index("tensor")
    xh, z = p // 8, p % 8
    y, xl, c = q // 4, (q // 2) % 2, q % 2

    def at(xh=xh, z=z, y=y, xl=xl, c=c):
        return place(xh, z, y, xl, c)

    up, down = at(z=(z + 1) % 8), at(z=(z + 7) % 8)
    core_peer = at(c=1 - c)
    xl_peer = at(xl=1 - xl)

    def local(source, target, i):
        return pltpu.make_async_copy(source, target, load_sem.at[i])

    loads = [local(grad_ref.at[:, h], blocks.at[7, h], h) for h in range(2)]
    loads.append(local(short_ref, weights.at[0], 2))
    loads.append(local(hidden_ref, hidden, 3))
    loads.append(local(hidden_ref.at[q], hidden_in.at[q], 4))
    loads.append(local(kv_ref, kv_all.at[q], 5))
    loads.append(local(down_ref.at[:, pl.ds(pl.multiple_of(q * 768, 128), 768)], down_rows, 6))
    loads.append(local(up_ref, up_rows, 7))
    for l in loads:
        l.start()

    barrier = pltpu.get_barrier_semaphore()

    def each(body, count=16):
        def step(d, carry):
            body(d)
            return carry
        lax.fori_loop(1, count, step, 0)

    def turn(a, d):
        return lax.rem(a + d, 16)

    def greet(d):
        pl.semaphore_signal(barrier, inc=1, device_id={"dp": p, "tensor": turn(q, d)}, device_id_type=MESH)
        pl.semaphore_signal(barrier, inc=1, device_id={"dp": turn(p, d), "tensor": q}, device_id_type=MESH)

    each(greet)

    @pl.when(p != q)
    def _():
        pl.semaphore_signal(barrier, inc=1, device_id={"dp": q, "tensor": p}, device_id_type=MESH)

    for l in loads:
        l.wait()

    @pl.when(p != q)
    def _():
        pl.semaphore_wait(barrier, 31)

    @pl.when(p == q)
    def _():
        pl.semaphore_wait(barrier, 30)

    def remote(src, dst, send, recv, to):
        return pltpu.make_async_remote_copy(
            src_ref=src, dst_ref=dst, send_sem=send, recv_sem=recv, device_id=to, device_id_type=MESH
        )

    def group(ref, sems):
        return remote(ref, ref, sems.at[0], sems.at[1], core_peer)

    def ring_copy(buffer, send, recv, s, h):
        source = 7 if s < 2 else (4 + h if s == 6 else s - 2)
        way = (up, down)[h if s == 6 else s % 2]
        return remote(buffer.at[source, h], buffer.at[s, h], send.at[0], recv.at[s, h], way)

    def block_copy(s, h):
        return ring_copy(blocks, a_send, a_recv, s, h)

    def w_copy(s, h):
        return ring_copy(w_ring, w_send, w_recv, s, h)

    def ring_step(copy, t):
        if t == 3:
            copy(6, 0).wait_recv()
            copy(6, 1).wait_recv()
            return
        for h in range(2):
            for s in (2 * t, 2 * t + 1):
                copy(s, h).wait_recv()
                if s < 4:
                    copy(s + 2, h).start()
                elif s - 4 == h:
                    copy(6, h).start()

    for h in range(2):
        for s in range(2):
            block_copy(s, h).start()

    def swap_copy():
        return remote(weights.at[0], weights.at[1], s_sem.at[0], s_sem.at[1], at(xh=1 - xh))

    swap_copy().start()

    def to_tensor(source, target, sems, d):
        return remote(source, target, sems.at[0], sems.at[1], {"dp": p, "tensor": turn(q, d)})

    def to_dp(source, target, sems, d):
        return remote(source, target, sems.at[0], sems.at[1], {"dp": turn(p, d), "tensor": q})

    def turn_copy(part):
        return remote(kvw_ref, w_ring.at[7, part], t_sem.at[0], t_sem.at[1], {"dp": q, "tensor": p})

    def turn_local():
        return pltpu.make_async_copy(kvw_ref, w_ring.at[7, xh], t_sem.at[0])

    def half_copy(part):
        return remote(w_ring.at[7, part], w_ring.at[7, part], t_sem.at[2], t_sem.at[3], at(xh=1 - xh))

    @pl.when(p != q)
    def _():
        turn_copy(q // 8).start()

    @pl.when(p == q)
    def _():
        turn_local().start()

    down_hi, down_lo = split(down_rows[...])
    mine = hidden[...].reshape(256, 768)
    low = contract(mine, jnp.concatenate([down_hi, down_lo], axis=0))
    wide = mine.astype(jnp.float32)
    squares = jnp.sum(wide * wide, axis=1, keepdims=True)
    sums = jnp.concatenate([low[:, :64] + low[:, 64:], jnp.broadcast_to(squares, (256, 64))], axis=1)
    sums_out[...] = sums.reshape(16, 16, 128)
    each(lambda d: to_tensor(sums_out.at[turn(q, d)], sums_in.at[q], su_sem, d).start())
    sums_in[q] = sums_out[q]
    each(lambda d: to_tensor(kv_ref, kv_all.at[q], k_sem, d).start())
    each(lambda d: to_tensor(hidden_ref.at[turn(q, d)], hidden_in.at[q], h_sem, d).start())

    def sums_reduce():
        group(sums_in.at[pl.ds(0, 15)], su_sem).wait_recv()
        sums_all[q] = jnp.sum(sums_in[...], axis=0)
        each(lambda d: to_tensor(sums_all.at[q], sums_all.at[q], sa_sem, d).start())

    def adapter_parts():
        group(sums_all.at[pl.ds(0, 15)], sa_sem).wait_recv()
        group(kv_all.at[pl.ds(0, 15)], k_sem).wait_recv()
        both = jnp.zeros((256, 128), jnp.float32)
        for s in range(16):
            hi, lo = split(up_rows[:, 128 * s : 128 * s + 128])
            both = both + contract(kv_all[s], jnp.concatenate([hi, lo], axis=0))
        back = both[:, :64] + both[:, 64:]
        back_keep[...] = back
        reduced = sums_all[...].reshape(256, 128)
        scale = lax.rsqrt(reduced[:, 64:65] / 12288 + epsilon)
        low = jnp.concatenate(split(scale * reduced[:, :64]), axis=1)
        upper = contract_first(low, kv_all[q])
        g_out[8:16, 24:32] = jnp.zeros((8, 8, 128), jnp.float32)
        g_out[0:8, 24:32] = (adapter_scale * (upper[:64] + upper[64:])).reshape(8, 8, 128)
        scaled = jnp.concatenate(split(scale * back), axis=1)
        lower = contract_first(scaled, hidden[...].reshape(256, 768))
        lower = adapter_scale * (lower[:64] + lower[64:])
        for b in range(6):
            g_rows[64 * b : 64 * b + 64] = lower[:, 128 * b : 128 * b + 128]
        g_out[:, 0:24] = g_rows[...].reshape(16, 24, 128)
        each(lambda d: to_dp(g_out.at[turn(p, d)], g_in.at[p], gs_sem, d).start())
        g_in[p] = g_out[p]

    def grads_reduce():
        group(g_in.at[pl.ds(0, 15)], gs_sem).wait_recv()
        g_all[q, p] = jnp.sum(g_in[...], axis=0).astype(jnp.bfloat16)
        each(lambda d: to_dp(g_all.at[q, p], g_all.at[q, p], gd_sem, d).start())

    def chips_copy(s, e):
        return remote(
            g_all.at[s], g_all.at[s], gt_send.at[0], gt_recv.at[e - 1], {"dp": p, "tensor": turn(q, 2 * e)}
        )

    def other_core_copy(s):
        return remote(g_all.at[s], g_all.at[s], gc_sem.at[0], gc_sem.at[1], core_peer)

    def grads_spread():
        group(g_all.at[q, pl.ds(0, 15)], gd_sem).wait_recv()
        each(lambda e: chips_copy(q, e).start(), 8)
        other_core_copy(q).start()

    def grads_forward():
        def body(e):
            s = turn(q, 16 - 2 * e)
            chips_copy(s, e).wait_recv()
            other_core_copy(s).start()
        each(body, 8)

    def block_z(s):
        half = (s + 2) // 2
        return lax.rem(z + 8 + jnp.where(s == 7, 0, jnp.where(s % 2 == 0, -half, half)), 8)

    def norm_term(slots):
        left = [kv_all[8 * part + block_z(s)] for s in slots for part in range(2)]
        right = [w_ring[s, part] for s in slots for part in range(2)]
        return contract(jnp.concatenate(left, axis=1), jnp.concatenate(right, axis=1))

    def norm_begin():
        half_copy(1 - xh).wait_recv()
        for h in range(2):
            for s in range(2):
                w_copy(s, h).start()

    def norm_hop(t):
        ring_step(w_copy, t)
        term = norm_term((2 * t, 2 * t + 1))
        norm_sum[...] = term if t == 0 else norm_sum[...] + term

    def norm_send():
        back_hi, back_lo = split(back_keep[...])
        down_hi, down_lo = split(down_rows[...])
        extra = multiply(
            jnp.concatenate([back_hi, back_lo], axis=1), jnp.concatenate([down_hi, down_hi], axis=0)
        ) + multiply(back_hi, down_lo)
        total = norm_sum[...] + adapter_scale * extra
        norm_out[...] = total.astype(jnp.bfloat16).reshape(16, 16, 768)
        each(lambda d: to_tensor(norm_out.at[turn(q, d)], norm_in.at[q], n_sem, d).start())
        norm_in[q] = norm_out[q]

    def turn_done():
        @pl.when(p != q)
        def _():
            turn_copy(xh).wait_recv()

        @pl.when(p == q)
        def _():
            turn_local().wait()

        half_copy(xh).start()

    def core_copy(i):
        return remote(core_out.at[i], core_in.at[i], core_send.at[0], core_recv.at[i], core_peer)

    def far_copy(i, way):
        return remote(
            y_out.at[i, (y + 2) % 4, way], far_in.at[i, way], far_send.at[0], far_recv.at[i, way],
            at(y=(y + 1 + 2 * way) % 4),
        )

    def near_copy(i, way):
        to = (y + 1 + 2 * way) % 4
        return remote(y_out.at[i, to], y_in.at[i, way], near_send.at[0], near_recv.at[i, way], at(y=to))

    def x_copy(i):
        return remote(x_out.at[i], x_in.at[i], x_send.at[0], x_recv.at[i], xl_peer)

    def fin_slot(i):
        g = i // 4
        return (xh + g - 2 * xh * g) * 8 + z

    before = {
        0: [lambda: ring_step(block_copy, 0)],
        1: [lambda: ring_step(block_copy, 1)],
        2: [lambda: ring_step(block_copy, 2)],
        3: [lambda: ring_step(block_copy, 3)],
        4: [lambda: swap_copy().wait_recv()],
    }
    after = {
        0: [turn_done],
        2: [norm_begin, sums_reduce],
        4: [adapter_parts],
        5: [lambda: norm_hop(0)],
        6: [grads_reduce],
        7: [lambda: norm_hop(1)],
        8: [grads_spread],
        9: [lambda: norm_hop(2)],
        10: [grads_forward],
        11: [lambda: norm_hop(3), norm_send],
    }

    def run(table, i):
        for when, acts in table.items():
            @pl.when(i == when)
            def _(acts=acts):
                for act in acts:
                    act()

    def step(i, carry):
        run(before, i)

        @pl.when(i < UNITS)
        def _():
            t, g = i % 4, i // 4
            both = contract(blocks[pl.ds(2 * t, 2)].reshape(512, 768), weights[g]).reshape(2, 2, 4, 32, 768)
            first, second = both[:, 0], both[:, 1]
            theirs = jnp.where(c == 0, second, first).astype(jnp.bfloat16)
            mine = jnp.where(c == 0, first, second)
            for b in range(2):
                core_out[i, :, b] = theirs[b]
            core_copy(i).start()
            for b in range(2):
                own[i, :, b] = mine[b]

        j = i - LAGS[0]

        @pl.when(jnp.logical_and(j >= 0, j < UNITS))
        def _():
            core_copy(j).wait_recv()
            total = own[j] + core_in[j].astype(jnp.float32)
            own[j] = total
            y_out[j] = total.astype(jnp.bfloat16)
            far_copy(j, 0).start()
            far_copy(j, 1).start()

        r = i - LAGS[1]

        @pl.when(jnp.logical_and(r >= 0, r < UNITS))
        def _():
            for way in range(2):
                far_copy(r, way).wait_recv()
                to = (y + 1 + 2 * way) % 4
                y_out[r, to, way] = (own[r, to, way] + far_in[r, way].astype(jnp.float32)).astype(jnp.bfloat16)
                near_copy(r, way).start()

        m = i - LAGS[2]

        @pl.when(jnp.logical_and(m >= 0, m < UNITS))
        def _():
            for way in range(2):
                near_copy(m, way).wait_recv()
            got = y_in[m].astype(jnp.float32)
            total = (own[m, y] + (got[0] + got[1])).reshape(2, 2, 16, 768)
            pair[m] = total
            for b in range(2):
                x_out[m, b] = pair[m, b, 1 - xl].astype(jnp.bfloat16)
            x_copy(m).start()

        n = i - LAGS[3]

        @pl.when(jnp.logical_and(n >= 0, n < UNITS))
        def _():
            x_copy(n).wait_recv()
            for b in range(2):
                done = (pair[n, b, xl] + x_in[n, b].astype(jnp.float32)).astype(jnp.bfloat16)
                s = 2 * (n % 4) + b
                slot = fin_slot(n)

                @pl.when(s == 7)
                def _():
                    fin_in[slot] = done

                @pl.when(s != 7)
                def _():
                    fin_out[n, b] = done
                    remote(
                        fin_out.at[n, b], fin_in.at[slot], f_sem.at[0], f_sem.at[1], at(z=block_z(s))
                    ).start()

        run(after, i)
        return carry

    lax.fori_loop(0, UNITS + LAGS[3], step, 0)

    group(g_all.at[pl.ds(0, 8)], gc_sem).wait_recv()

    def unpack(s, carry):
        packed = g_all[s].astype(jnp.float32)
        lower = packed[:, :24].reshape(6, 64, 128)
        for b in range(6):
            down_out[:, pl.ds(pl.multiple_of(s * 768 + 128 * b, 128), 128)] = lower[b].astype(down_out.dtype)
        up_out[:, pl.ds(pl.multiple_of(s * 128, 128), 128)] = packed[:8, 24:].reshape(64, 128).astype(up_out.dtype)
        return carry

    lax.fori_loop(0, 16, unpack, 0)

    group(hidden_in.at[pl.ds(0, 15)], h_sem).wait_recv()
    group(norm_in.at[pl.ds(0, 15)], n_sem).wait_recv()
    my_scale = lax.rsqrt(sums_all[q][:, 64:65] / 12288 + epsilon)

    def dots(s, total):
        return total + hidden_in[s].astype(jnp.float32) * norm_in[s].astype(jnp.float32)

    products = lax.fori_loop(0, 16, dots, jnp.zeros((16, 768), jnp.float32))
    inner = jnp.sum(products, axis=1, keepdims=True) * my_scale / 12288
    group(fin_in.at[pl.ds(0, 14)], f_sem).wait_recv()

    def take(s, carry):
        normed = hidden_in[s].astype(jnp.float32) * my_scale
        done = fin_in[s].astype(jnp.float32) + my_scale * (norm_in[s].astype(jnp.float32) - normed * inner)
        out_ref[:, pl.ds(pl.multiple_of(s * 768, 128), 768)] = done.astype(out_ref.dtype)
        return carry

    lax.fori_loop(0, 16, take, 0)

    def gone(ref, sems):
        remote(ref, ref, sems.at[0], sems.at[0], core_peer).wait_send()

    gone(blocks.at[pl.ds(0, 7)], a_send)
    gone(w_ring.at[pl.ds(0, 7)], w_send)
    swap_copy().wait_send()
    gone(core_out, core_send)
    gone(far_in, far_send)
    gone(y_in, near_send)
    gone(x_out, x_send)
    gone(fin_in.at[pl.ds(0, 14)], f_sem)
    half_copy(xh).wait_send()

    @pl.when(p != q)
    def _():
        turn_copy(q // 8).wait_send()

    gone(sums_in.at[pl.ds(0, 15)], su_sem)
    gone(sums_all.at[pl.ds(0, 15)], sa_sem)
    gone(kv_all.at[pl.ds(0, 15)], k_sem)
    gone(hidden_in.at[pl.ds(0, 15)], h_sem)
    gone(norm_in.at[pl.ds(0, 15)], n_sem)
    gone(g_in.at[pl.ds(0, 15)], gs_sem)
    gone(g_all.at[0, pl.ds(0, 15)], gd_sem)
    gone(g_all.at[pl.ds(0, 7)], gt_send)
    gone(g_all.at[pl.ds(0, 8)], gc_sem)


def shards(hidden_in, residual_grad, key_value_gradient, shortcut, key_value_weight, adapter_down_matrix, adapter_up):
    bf, f32, dma = jnp.bfloat16, jnp.float32, pltpu.SemaphoreType.DMA
    v = pltpu.VMEM
    result, down, up = pl.pallas_call(
        whole_kernel,
        out_shape=[
            jax.ShapeDtypeStruct((16, 12288), bf),
            jax.ShapeDtypeStruct((64, 12288), bf),
            jax.ShapeDtypeStruct((64, 2048), bf),
        ],
        in_specs=[pl.BlockSpec(memory_space=pl.ANY)] * 7,
        out_specs=[pl.BlockSpec(memory_space=pltpu.VMEM)] * 3,
        scratch_shapes=[
            v((8, 2, 8, 16, 768), bf), v((2, 768, 768), bf),
            v((UNITS, 4, 2, 32, 768), bf), v((UNITS, 4, 2, 32, 768), bf), v((UNITS, 4, 2, 32, 768), f32),
            v((UNITS, 4, 2, 32, 768), bf), v((UNITS, 2, 32, 768), bf), v((UNITS, 2, 2, 32, 768), bf),
            v((UNITS, 2, 2, 16, 768), f32), v((UNITS, 2, 16, 768), bf), v((UNITS, 2, 16, 768), bf),
            v((UNITS, 2, 16, 768), bf), v((16, 16, 768), bf),
            v((16, 16, 768), bf), v((16, 16, 768), bf), v((16, 256, 128), bf), v((8, 2, 768, 128), bf),
            v((64, 768), f32), v((64, 2048), f32), v((16, 16, 128), f32), v((16, 16, 128), f32),
            v((16, 16, 128), f32), v((256, 64), f32),
            v((256, 768), f32), v((16, 16, 768), bf), v((16, 16, 768), bf),
            v((16, 32, 128), f32), v((16, 32, 128), f32), v((16, 16, 32, 128), bf), v((384, 128), f32),
            dma((8,)), dma((1,)), dma((7, 2)), dma((2,)),
            dma((1,)), dma((UNITS,)), dma((1,)), dma((UNITS, 2)), dma((1,)), dma((UNITS, 2)),
            dma((1,)), dma((UNITS,)), dma((2,)),
            *[dma((2,))] * 7, dma((1,)), dma((7,)), dma((2,)), dma((4,)), dma((1,)), dma((7, 2)),
        ],
        compiler_params=pltpu.CompilerParams(
            collective_id=0, has_side_effects=True, vmem_limit_bytes=58 * 1024 * 1024
        ),
        cost_estimate=pl.CostEstimate(flops=5_900_000_000, bytes_accessed=12_000_000, transcendentals=512),
    )(
        residual_grad.reshape(8, 2, 16, 768), shortcut, hidden_in.reshape(16, 16, 768), key_value_gradient,
        key_value_weight, adapter_down_matrix.T, adapter_up,
    )
    return result, down.astype(f32).T, up.astype(f32)


def solution(mesh):
    part = P("dp", "tensor")
    return jax.shard_map(
        shards, mesh=mesh, in_specs=(part,) * 5 + (P(), P()),
        out_specs=(P(("dp", "tensor"), None), P(), P()), check_vma=False,
    )
```

time: 938 us -> 136 us (0.14)
  waiting for transfers between devices: 825 us -> 0 us
  Pallas kernels: 0 us -> 130 us
  matrix products: 31.4 us -> 0 us
  blocking collectives: 30 us -> 0 us
  other arithmetic: 20.5 us -> 4.17 us
  between operations: 15.7 us -> 0.66 us
    all_gather x2 -> x0, waiting for transfers between devices: 335 us -> none  [the longest x1 243 us: shards(): lax.all_gather(shortcut, 'dp', axis=0, tiled=True)]
    psum x2 -> x0, waiting for transfers between devices: 266 us -> none  [the longest x1 266 us: shards(): lax.psum((down_full, up_full), ('dp', 'tensor'))]
    reduce_scatter x1 -> x0, waiting for transfers between devices: 223 us -> none  [shards(): lax.psum_scatter(jnp.concatenate([shortcut_term, norm_term], axis=1), 'te...]
    pallas_call x0 -> x1, Pallas kernels: none -> 130 us  [shards(): pl.pallas_call(whole_kernel, out_shape=[jax.ShapeDtypeStruct((16, 12288),...]
    dot_general x7 -> x0, matrix products: 31.4 us -> none  [the longest x2 20 us: contract_final_axis(): lax.dot_general(left, right, (((1,), (1,)), ((), ())), preferred_element_...]
    psum x1 -> x0, blocking collectives: 30 us -> none  [shards(): lax.psum((partial_down, partial_back, partial_squares), 'tensor')]
    concatenate x1 -> x0, other arithmetic: 18.3 us -> none  [shards(): jnp.concatenate([shortcut_term, norm_term], axis=1)]
  transfers between devices with their start and end apart: 6 -> 0, of which waited for: 4 -> 0; matrix products, arithmetic and copies ran while one was open for 6% -> 0% of each run, Pallas kernels for 0% -> 0%
where the time goes in v3:
time: 136 us
  Pallas kernels  130 us (96%)
  other arithmetic  4.17 us (3%)
    pallas_call x1, Pallas kernels, shards(): pl.pallas_call(whole_kernel, out_shape=[jax.ShapeDtypeStruct((16, 12288),...  130 us
    transpose x1, other arithmetic, shards(): return (result, down.astype(f32).T, up.astype(f32))  3.34 us

profile of v3, /device:TPU:1, one launch (start us, length us, event | category | flops | bytes accessed | tf_op | source)
XLA Modules:
  0.0 135.8 jit_solution(70133017703568608)
XLA Ops:
  0.6 130.2 %shard_map.94 = (bf16[16,12288]{1,0:T(8,128)(2,1)}, bf16[64,12288]{1,0:T(8,128)(2,1)}, bf16[64,2048]{1,0:T(8,128)(2,1)}) custom-call(bf16[8,2,16,768]{3,2,1,0:T(8,128)(2,1)} %bitcast.6, bf16[768,768]{1,0:T(8,128)(2,1)} %short_ref.1, bf16[16,16,768]{2,1,0:T(8,128)(2,1)} %bitcast.7, bf16[256,128]{1,0:T(8,128)(2,1)} %kv_ref.1, bf16[768,128]{1,0:T(8,128)(2,1)} %kvw_ref.1, ...), custom_call_target="tpu_custom_call" | custom-call | flops 5900000256 | bytes 12000000 | tf_op jit(solution)/shard_map/pallas_call | solution.py:459
  130.8 0.0 copy-start.1
  130.9 0.0 copy-start
  130.9 3.3 %convert_bitcast_fusion = f32[12288,64]{0,1:T(8,128)} fusion(bf16[64,12288]{1,0:T(8,128)(2,1)} %get-tuple-element.7), kind=kLoop, calls=%fused_computation | loop fusion | flops 786432 | bytes 4718592 | tf_op jit(solution)/shard_map/transpose | solution.py:492
  134.2 0.0 copy-done.1
  134.2 0.8 convert_element_type.4
  135.0 0.0 copy-done
  135.0 0.7 copy.11
Async XLA Ops:
  130.8 3.4 %copy-start.1 = (bf16[64,2048]{1,0:T(8,128)(2,1)S(1)}, bf16[64,2048]{1,0:T(8,128)(2,1)}, u32[]{:S(2)}) copy-start(bf16[64,2048]{1,0:T(8,128)(2,1)} %get-tuple-element.8) | copy-start | bytes 786436
  130.9 4.2 %copy-start = (bf16[16,12288]{1,0:T(8,128)(2,1)S(1)}, bf16[16,12288]{1,0:T(8,128)(2,1)}, u32[]{:S(2)}) copy-start(bf16[16,12288]{1,0:T(8,128)(2,1)} %get-tuple-element.12) | copy-start | bytes 1179652

commit v4 on v3

--- a/solution.py
+++ b/solution.py
@@ -7,7 +7,7 @@
 
 MESH = pl.DeviceIdType.MESH
 UNITS = 8
-LAGS = (1, 2, 3, 4)
+LAGS = (1, 2, 4, 5)
 epsilon = 1e-05
 adapter_scale = 0.25
 
@@ -41,7 +41,7 @@
     norm_sum, norm_out, norm_in, g_out, g_in, g_all, g_rows,
     load_sem, a_send, a_recv, s_sem,
     core_send, core_recv, far_send, far_recv, near_send, near_recv, x_send, x_recv, f_sem,
-    h_sem, k_sem, su_sem, sa_sem, n_sem, gs_sem, gd_sem, gt_send, gt_recv, gc_sem, t_sem, w_send, w_recv,
+    h_sem, k_sem, kc_sem, su_sem, sa_sem, n_sem, gs_sem, gd_sem, gt_send, gt_recv, gc_sem, t_sem, w_send, w_recv,
 ):
     p, q = lax.axis_index("dp"), lax.axis_index("tensor")
     xh, z = p // 8, p % 8
@@ -61,7 +61,7 @@
     loads.append(local(short_ref, weights.at[0], 2))
     loads.append(local(hidden_ref, hidden, 3))
     loads.append(local(hidden_ref.at[q], hidden_in.at[q], 4))
-    loads.append(local(kv_ref, kv_all.at[q], 5))
+    loads.append(local(kv_ref, kv_all.at[q // 2, c], 5))
     loads.append(local(down_ref.at[:, pl.ds(pl.multiple_of(q * 768, 128), 768)], down_rows, 6))
     loads.append(local(up_ref, up_rows, 7))
     for l in loads:
@@ -118,18 +118,20 @@
     def w_copy(s, h):
         return ring_copy(w_ring, w_send, w_recv, s, h)
 
+    def ring_half(copy, t, h):
+        if t == 3:
+            copy(6, h).wait_recv()
+            return
+        for s in (2 * t, 2 * t + 1):
+            copy(s, h).wait_recv()
+            if s < 4:
+                copy(s + 2, h).start()
+            elif s - 4 == h:
+                copy(6, h).start()
+
     def ring_step(copy, t):
-        if t == 3:
-            copy(6, 0).wait_recv()
-            copy(6, 1).wait_recv()
-            return
-        for h in range(2):
-            for s in (2 * t, 2 * t + 1):
-                copy(s, h).wait_recv()
-                if s < 4:
-                    copy(s + 2, h).start()
-                elif s - 4 == h:
-                    copy(6, h).start()
+        ring_half(copy, t, 0)
+        ring_half(copy, t, 1)
 
     for h in range(2):
         for s in range(2):
@@ -172,8 +174,19 @@
     sums_out[...] = sums.reshape(16, 16, 128)
     each(lambda d: to_tensor(sums_out.at[turn(q, d)], sums_in.at[q], su_sem, d).start())
     sums_in[q] = sums_out[q]
-    each(lambda d: to_tensor(kv_ref, kv_all.at[q], k_sem, d).start())
-    each(lambda d: to_tensor(hidden_ref.at[turn(q, d)], hidden_in.at[q], h_sem, d).start())
+
+    def kv_send():
+        each(lambda e: to_tensor(kv_ref, kv_all.at[q // 2, c], k_sem, 2 * e).start(), 8)
+
+    def kv_core_copy():
+        return remote(kv_all.at[:, c], kv_all.at[:, c], kc_sem.at[0], kc_sem.at[1], core_peer)
+
+    def kv_forward():
+        group(kv_all.at[pl.ds(0, 7), 0], k_sem).wait_recv()
+        kv_core_copy().start()
+
+    def hidden_send():
+        each(lambda d: to_tensor(hidden_ref.at[turn(q, d)], hidden_in.at[q], h_sem, d).start())
 
     def sums_reduce():
         group(sums_in.at[pl.ds(0, 15)], su_sem).wait_recv()
@@ -182,17 +195,17 @@
 
     def adapter_parts():
         group(sums_all.at[pl.ds(0, 15)], sa_sem).wait_recv()
-        group(kv_all.at[pl.ds(0, 15)], k_sem).wait_recv()
+        kv_core_copy().wait_recv()
         both = jnp.zeros((256, 128), jnp.float32)
         for s in range(16):
             hi, lo = split(up_rows[:, 128 * s : 128 * s + 128])
-            both = both + contract(kv_all[s], jnp.concatenate([hi, lo], axis=0))
+            both = both + contract(kv_all[s // 2, s % 2], jnp.concatenate([hi, lo], axis=0))
         back = both[:, :64] + both[:, 64:]
         back_keep[...] = back
         reduced = sums_all[...].reshape(256, 128)
         scale = lax.rsqrt(reduced[:, 64:65] / 12288 + epsilon)
         low = jnp.concatenate(split(scale * reduced[:, :64]), axis=1)
-        upper = contract_first(low, kv_all[q])
+        upper = contract_first(low, kv_all[q // 2, c])
         g_out[8:16, 24:32] = jnp.zeros((8, 8, 128), jnp.float32)
         g_out[0:8, 24:32] = (adapter_scale * (upper[:64] + upper[64:])).reshape(8, 8, 128)
         scaled = jnp.concatenate(split(scale * back), axis=1)
@@ -234,7 +247,7 @@
         return lax.rem(z + 8 + jnp.where(s == 7, 0, jnp.where(s % 2 == 0, -half, half)), 8)
 
     def norm_term(slots):
-        left = [kv_all[8 * part + block_z(s)] for s in slots for part in range(2)]
+        left = [kv_all[4 * part + block_z(s) // 2, block_z(s) % 2] for s in slots for part in range(2)]
         right = [w_ring[s, part] for s in slots for part in range(2)]
         return contract(jnp.concatenate(left, axis=1), jnp.concatenate(right, axis=1))
 
@@ -244,8 +257,11 @@
             for s in range(2):
                 w_copy(s, h).start()
 
+    def norm_half(t):
+        ring_half(w_copy, t, 0)
+
     def norm_hop(t):
-        ring_step(w_copy, t)
+        ring_half(w_copy, t, 1)
         term = norm_term((2 * t, 2 * t + 1))
         norm_sum[...] = term if t == 0 else norm_sum[...] + term
 
@@ -287,27 +303,35 @@
     def x_copy(i):
         return remote(x_out.at[i], x_in.at[i], x_send.at[0], x_recv.at[i], xl_peer)
 
+    def side_of(i):
+        return jnp.where(i > 4, 1, jnp.where(i == 3, 1, 0))
+
+    def pair_of(i):
+        return jnp.where(i > 4, i - 4, jnp.where(i == 4, 3, jnp.where(i == 3, 0, i)))
+
     def fin_slot(i):
-        g = i // 4
+        g = side_of(i)
         return (xh + g - 2 * xh * g) * 8 + z
 
     before = {
         0: [lambda: ring_step(block_copy, 0)],
         1: [lambda: ring_step(block_copy, 1)],
         2: [lambda: ring_step(block_copy, 2)],
-        3: [lambda: ring_step(block_copy, 3)],
-        4: [lambda: swap_copy().wait_recv()],
+        3: [lambda: swap_copy().wait_recv()],
+        4: [lambda: ring_step(block_copy, 3)],
     }
     after = {
-        0: [turn_done],
-        2: [norm_begin, sums_reduce],
-        4: [adapter_parts],
+        0: [turn_done, kv_send],
+        1: [sums_reduce],
+        2: [norm_begin, kv_forward],
+        3: [hidden_send],
+        4: [adapter_parts, lambda: norm_half(0)],
         5: [lambda: norm_hop(0)],
-        6: [grads_reduce],
+        6: [grads_reduce, lambda: norm_half(1)],
         7: [lambda: norm_hop(1)],
-        8: [grads_spread],
+        8: [grads_spread, lambda: norm_half(2)],
         9: [lambda: norm_hop(2)],
-        10: [grads_forward],
+        10: [lambda: norm_half(3), grads_forward],
         11: [lambda: norm_hop(3), norm_send],
     }
 
@@ -323,7 +347,7 @@
 
         @pl.when(i < UNITS)
         def _():
-            t, g = i % 4, i // 4
+            t, g = pair_of(i), side_of(i)
             both = contract(blocks[pl.ds(2 * t, 2)].reshape(512, 768), weights[g]).reshape(2, 2, 4, 32, 768)
             first, second = both[:, 0], both[:, 1]
             theirs = jnp.where(c == 0, second, first).astype(jnp.bfloat16)
@@ -375,7 +399,7 @@
             x_copy(n).wait_recv()
             for b in range(2):
                 done = (pair[n, b, xl] + x_in[n, b].astype(jnp.float32)).astype(jnp.bfloat16)
-                s = 2 * (n % 4) + b
+                s = 2 * pair_of(n) + b
                 slot = fin_slot(n)
 
                 @pl.when(s == 7)
@@ -444,7 +468,8 @@
 
     gone(sums_in.at[pl.ds(0, 15)], su_sem)
     gone(sums_all.at[pl.ds(0, 15)], sa_sem)
-    gone(kv_all.at[pl.ds(0, 15)], k_sem)
+    gone(kv_all.at[pl.ds(0, 7), 0], k_sem)
+    kv_core_copy().wait_send()
     gone(hidden_in.at[pl.ds(0, 15)], h_sem)
     gone(norm_in.at[pl.ds(0, 15)], n_sem)
     gone(g_in.at[pl.ds(0, 15)], gs_sem)
@@ -471,7 +496,7 @@
             v((UNITS, 4, 2, 32, 768), bf), v((UNITS, 2, 32, 768), bf), v((UNITS, 2, 2, 32, 768), bf),
             v((UNITS, 2, 2, 16, 768), f32), v((UNITS, 2, 16, 768), bf), v((UNITS, 2, 16, 768), bf),
             v((UNITS, 2, 16, 768), bf), v((16, 16, 768), bf),
-            v((16, 16, 768), bf), v((16, 16, 768), bf), v((16, 256, 128), bf), v((8, 2, 768, 128), bf),
+            v((16, 16, 768), bf), v((16, 16, 768), bf), v((8, 2, 256, 128), bf), v((8, 2, 768, 128), bf),
             v((64, 768), f32), v((64, 2048), f32), v((16, 16, 128), f32), v((16, 16, 128), f32),
             v((16, 16, 128), f32), v((256, 64), f32),
             v((256, 768), f32), v((16, 16, 768), bf), v((16, 16, 768), bf),
@@ -479,7 +504,7 @@
             dma((8,)), dma((1,)), dma((7, 2)), dma((2,)),
             dma((1,)), dma((UNITS,)), dma((1,)), dma((UNITS, 2)), dma((1,)), dma((UNITS, 2)),
             dma((1,)), dma((UNITS,)), dma((2,)),
-            *[dma((2,))] * 7, dma((1,)), dma((7,)), dma((2,)), dma((4,)), dma((1,)), dma((7, 2)),
+            *[dma((2,))] * 8, dma((1,)), dma((7,)), dma((2,)), dma((4,)), dma((1,)), dma((7, 2)),
         ],
         compiler_params=pltpu.CompilerParams(
             collective_id=0, has_side_effects=True, vmem_limit_bytes=58 * 1024 * 1024

time: 136 us -> 123 us (0.904); the launches traced: 136 us -> 121 us
  Pallas kernels: 130 us -> 116 us
    pallas_call x1, Pallas kernels: 130 us -> 116 us  [shards(): pl.pallas_call(whole_kernel, out_shape=[jax.ShapeDtypeStruct((16, 12288),...]
where the time goes in v4:
time: 123 us; the launch traced here: 121 us
  Pallas kernels  116 us (94%)
  other arithmetic  4.17 us (3%)
    pallas_call x1, Pallas kernels, shards(): pl.pallas_call(whole_kernel, out_shape=[jax.ShapeDtypeStruct((16, 12288),...  116 us
    transpose x1, other arithmetic, shards(): return (result, down.astype(f32).T, up.astype(f32))  3.34 us

profile of v4, /device:TPU:1, one launch (start us, length us, event | category | flops | bytes accessed | tf_op | source)
XLA Modules:
  0.0 121.4 jit_solution(15565782029494139887)
XLA Ops:
  0.6 115.8 %shard_map.94 = (bf16[16,12288]{1,0:T(8,128)(2,1)}, bf16[64,12288]{1,0:T(8,128)(2,1)}, bf16[64,2048]{1,0:T(8,128)(2,1)}) custom-call(bf16[8,2,16,768]{3,2,1,0:T(8,128)(2,1)} %bitcast.6, bf16[768,768]{1,0:T(8,128)(2,1)} %short_ref.1, bf16[16,16,768]{2,1,0:T(8,128)(2,1)} %bitcast.7, bf16[256,128]{1,0:T(8,128)(2,1)} %kv_ref.1, bf16[768,128]{1,0:T(8,128)(2,1)} %kvw_ref.1, ...), custom_call_target="tpu_custom_call" | custom-call | flops 5900000256 | bytes 12000000 | tf_op jit(solution)/shard_map/pallas_call | solution.py:484
  116.4 0.0 copy-start.1
  116.4 0.0 copy-start
  116.4 3.3 %convert_bitcast_fusion = f32[12288,64]{0,1:T(8,128)} fusion(bf16[64,12288]{1,0:T(8,128)(2,1)} %get-tuple-element.7), kind=kLoop, calls=%fused_computation | loop fusion | flops 786432 | bytes 4718592 | tf_op jit(solution)/shard_map/transpose | solution.py:517
  119.8 0.0 copy-done.1
  119.8 0.8 convert_element_type.4
  120.6 0.0 copy-done
  120.6 0.7 copy.11
Async XLA Ops:
  116.4 3.4 %copy-start.1 = (bf16[64,2048]{1,0:T(8,128)(2,1)S(1)}, bf16[64,2048]{1,0:T(8,128)(2,1)}, u32[]{:S(2)}) copy-start(bf16[64,2048]{1,0:T(8,128)(2,1)} %get-tuple-element.8) | copy-start | bytes 786436
  116.4 4.2 %copy-start = (bf16[16,12288]{1,0:T(8,128)(2,1)S(1)}, bf16[16,12288]{1,0:T(8,128)(2,1)}, u32[]{:S(2)}) copy-start(bf16[16,12288]{1,0:T(8,128)(2,1)} %get-tuple-element.12) | copy-start | bytes 1179652

commit v5 on v4

--- a/solution.py
+++ b/solution.py
@@ -7,7 +7,7 @@
 
 MESH = pl.DeviceIdType.MESH
 UNITS = 8
-LAGS = (1, 2, 4, 5)
+LAGS = (1, 2, 4, 6)
 epsilon = 1e-05
 adapter_scale = 0.25
 
@@ -38,7 +38,7 @@
     out_ref, down_out, up_out,
     blocks, weights, core_out, core_in, own, y_out, far_in, y_in, pair, x_out, x_in, fin_out, fin_in,
     hidden, hidden_in, kv_all, w_ring, down_rows, up_rows, sums_out, sums_in, sums_all, back_keep,
-    norm_sum, norm_out, norm_in, g_out, g_in, g_all, g_rows,
+    norm_sum, norm_out, norm_in, g_out, g_wire, g_in, g_all, g_rows,
     load_sem, a_send, a_recv, s_sem,
     core_send, core_recv, far_send, far_recv, near_send, near_recv, x_send, x_recv, f_sem,
     h_sem, k_sem, kc_sem, su_sem, sa_sem, n_sem, gs_sem, gd_sem, gt_send, gt_recv, gc_sem, t_sem, w_send, w_recv,
@@ -214,12 +214,13 @@
         for b in range(6):
             g_rows[64 * b : 64 * b + 64] = lower[:, 128 * b : 128 * b + 128]
         g_out[:, 0:24] = g_rows[...].reshape(16, 24, 128)
-        each(lambda d: to_dp(g_out.at[turn(p, d)], g_in.at[p], gs_sem, d).start())
-        g_in[p] = g_out[p]
+        g_wire[...] = g_out[...].astype(jnp.bfloat16)
+        each(lambda d: to_dp(g_wire.at[turn(p, d)], g_in.at[p], gs_sem, d).start())
+        g_in[p] = g_wire[p]
 
     def grads_reduce():
         group(g_in.at[pl.ds(0, 15)], gs_sem).wait_recv()
-        g_all[q, p] = jnp.sum(g_in[...], axis=0).astype(jnp.bfloat16)
+        g_all[q, p] = jnp.sum(g_in[...].astype(jnp.float32), axis=0).astype(jnp.bfloat16)
         each(lambda d: to_dp(g_all.at[q, p], g_all.at[q, p], gd_sem, d).start())
 
     def chips_copy(s, e):
@@ -322,9 +323,8 @@
     }
     after = {
         0: [turn_done, kv_send],
-        1: [sums_reduce],
+        1: [sums_reduce, hidden_send],
         2: [norm_begin, kv_forward],
-        3: [hidden_send],
         4: [adapter_parts, lambda: norm_half(0)],
         5: [lambda: norm_hop(0)],
         6: [grads_reduce, lambda: norm_half(1)],
@@ -500,7 +500,7 @@
             v((64, 768), f32), v((64, 2048), f32), v((16, 16, 128), f32), v((16, 16, 128), f32),
             v((16, 16, 128), f32), v((256, 64), f32),
             v((256, 768), f32), v((16, 16, 768), bf), v((16, 16, 768), bf),
-            v((16, 32, 128), f32), v((16, 32, 128), f32), v((16, 16, 32, 128), bf), v((384, 128), f32),
+            v((16, 32, 128), f32), v((16, 32, 128), bf), v((16, 32, 128), bf), v((16, 16, 32, 128), bf), v((384, 128), f32),
             dma((8,)), dma((1,)), dma((7, 2)), dma((2,)),
             dma((1,)), dma((UNITS,)), dma((1,)), dma((UNITS, 2)), dma((1,)), dma((UNITS, 2)),
             dma((1,)), dma((UNITS,)), dma((2,)),

time: 123 us -> 118 us (0.959); the launches traced: 121 us -> 118 us
  Pallas kernels: 116 us -> 112 us
    pallas_call x1, Pallas kernels: 116 us -> 112 us  [shards(): pl.pallas_call(whole_kernel, out_shape=[jax.ShapeDtypeStruct((16, 12288),...]
where the time goes in v5:
time: 118 us
  Pallas kernels  112 us (95%)
  other arithmetic  4.17 us (4%)
    pallas_call x1, Pallas kernels, shards(): pl.pallas_call(whole_kernel, out_shape=[jax.ShapeDtypeStruct((16, 12288),...  112 us
    transpose x1, other arithmetic, shards(): return (result, down.astype(f32).T, up.astype(f32))  3.34 us

profile of v5, /device:TPU:1, one launch (start us, length us, event | category | flops | bytes accessed | tf_op | source)
XLA Modules:
  0.0 117.8 jit_solution(8122233027687226490)
XLA Ops:
  0.6 112.2 %shard_map.94 = (bf16[16,12288]{1,0:T(8,128)(2,1)}, bf16[64,12288]{1,0:T(8,128)(2,1)}, bf16[64,2048]{1,0:T(8,128)(2,1)}) custom-call(bf16[8,2,16,768]{3,2,1,0:T(8,128)(2,1)} %bitcast.6, bf16[768,768]{1,0:T(8,128)(2,1)} %short_ref.1, bf16[16,16,768]{2,1,0:T(8,128)(2,1)} %bitcast.7, bf16[256,128]{1,0:T(8,128)(2,1)} %kv_ref.1, bf16[768,128]{1,0:T(8,128)(2,1)} %kvw_ref.1, ...), custom_call_target="tpu_custom_call" | custom-call | flops 5900000256 | bytes 12000000 | tf_op jit(solution)/shard_map/pallas_call | solution.py:484
  112.8 0.0 copy-start.1
  112.8 0.0 copy-start
  112.9 3.3 %convert_bitcast_fusion = f32[12288,64]{0,1:T(8,128)} fusion(bf16[64,12288]{1,0:T(8,128)(2,1)} %get-tuple-element.7), kind=kLoop, calls=%fused_computation | loop fusion | flops 786432 | bytes 4718592 | tf_op jit(solution)/shard_map/transpose | solution.py:517
  116.2 0.0 copy-done.1
  116.2 0.8 convert_element_type.4
  117.0 0.0 copy-done
  117.0 0.7 copy.11
Async XLA Ops:
  112.8 3.4 %copy-start.1 = (bf16[64,2048]{1,0:T(8,128)(2,1)S(1)}, bf16[64,2048]{1,0:T(8,128)(2,1)}, u32[]{:S(2)}) copy-start(bf16[64,2048]{1,0:T(8,128)(2,1)} %get-tuple-element.8) | copy-start | bytes 786436
  112.8 4.2 %copy-start = (bf16[16,12288]{1,0:T(8,128)(2,1)S(1)}, bf16[16,12288]{1,0:T(8,128)(2,1)}, u32[]{:S(2)}) copy-start(bf16[16,12288]{1,0:T(8,128)(2,1)} %get-tuple-element.12) | copy-start | bytes 1179652

commit v6 on v5

--- a/solution.py
+++ b/solution.py
@@ -322,8 +322,8 @@
         4: [lambda: ring_step(block_copy, 3)],
     }
     after = {
-        0: [turn_done, kv_send],
-        1: [sums_reduce, hidden_send],
+        0: [turn_done, kv_send, hidden_send],
+        1: [sums_reduce],
         2: [norm_begin, kv_forward],
         4: [adapter_parts, lambda: norm_half(0)],
         5: [lambda: norm_hop(0)],

time: 118 us -> 119 us (level)
  no operation moved by 1% of the time
where the time goes in v6:
time: 119 us
  Pallas kernels  113 us (95%)
  other arithmetic  4.17 us (4%)
    pallas_call x1, Pallas kernels, shards(): pl.pallas_call(whole_kernel, out_shape=[jax.ShapeDtypeStruct((16, 12288),...  113 us
    transpose x1, other arithmetic, shards(): return (result, down.astype(f32).T, up.astype(f32))  3.34 us

profile of v6, /device:TPU:1, one launch (start us, length us, event | category | flops | bytes accessed | tf_op | source)
XLA Modules:
  0.0 118.8 jit_solution(16466165320559041156)
XLA Ops:
  0.6 113.2 %shard_map.94 = (bf16[16,12288]{1,0:T(8,128)(2,1)}, bf16[64,12288]{1,0:T(8,128)(2,1)}, bf16[64,2048]{1,0:T(8,128)(2,1)}) custom-call(bf16[8,2,16,768]{3,2,1,0:T(8,128)(2,1)} %bitcast.6, bf16[768,768]{1,0:T(8,128)(2,1)} %short_ref.1, bf16[16,16,768]{2,1,0:T(8,128)(2,1)} %bitcast.7, bf16[256,128]{1,0:T(8,128)(2,1)} %kv_ref.1, bf16[768,128]{1,0:T(8,128)(2,1)} %kvw_ref.1, ...), custom_call_target="tpu_custom_call" | custom-call | flops 5900000256 | bytes 12000000 | tf_op jit(solution)/shard_map/pallas_call | solution.py:484
  113.8 0.0 copy-start.1
  113.9 0.0 copy-start
  113.9 3.3 %convert_bitcast_fusion = f32[12288,64]{0,1:T(8,128)} fusion(bf16[64,12288]{1,0:T(8,128)(2,1)} %get-tuple-element.7), kind=kLoop, calls=%fused_computation | loop fusion | flops 786432 | bytes 4718592 | tf_op jit(solution)/shard_map/transpose | solution.py:517
  117.2 0.0 copy-done.1
  117.2 0.8 convert_element_type.4
  118.0 0.0 copy-done
  118.0 0.7 copy.11
Async XLA Ops:
  113.8 3.4 %copy-start.1 = (bf16[64,2048]{1,0:T(8,128)(2,1)S(1)}, bf16[64,2048]{1,0:T(8,128)(2,1)}, u32[]{:S(2)}) copy-start(bf16[64,2048]{1,0:T(8,128)(2,1)} %get-tuple-element.8) | copy-start | bytes 786436
  113.9 4.2 %copy-start = (bf16[16,12288]{1,0:T(8,128)(2,1)S(1)}, bf16[16,12288]{1,0:T(8,128)(2,1)}, u32[]{:S(2)}) copy-start(bf16[16,12288]{1,0:T(8,128)(2,1)} %get-tuple-element.12) | copy-start | bytes 1179652
